TPU v7x, 128 devices: a whole 4x4x4 slice. The times are simulated.
128 devices in a mesh: row: 8 (over y, core), col: 16 (over z, x).
Axes of the slice: x: 4, y: 4, z: 4, core: 2. Of those that a mesh axis runs over, the one named last changes fastest.
Arguments:
- front: float32 [12288, 12288], P('row', 'col'), may hold values from -6 to 6
- delayed: float32 [128, 12288], P('col', 'row'), may hold values from -6 to 6
- dest: int32 [128], P('col'), may hold values from 0 to 1023, as said below
- pivots: int32 [1024], replicated, may hold values from 0 to 12287, as said below
- pair_flags: int32 [1024], replicated, may hold values from 0 to 1, as said below
- linv: float32 [4, 256, 256], replicated, as said below
- dinv_diag: float32 [1024], replicated, may hold values from -0.1 to 0.1
- dinv_off: float32 [1024], replicated, may hold values from -0.08 to 0.08
Outputs:
- trailing: float32 [12288, 12288], P('row', 'col')
- factor: float32 [12288, 1024], P('row')
Inputs may be any that keep to these rules, and one draw needn't show every extreme that they name: Distinct front columns; slots p * 256 to (p + 1) * 256 - 1 are panel p's pivots. Each block of 768 columns held by one index of col contains exactly 64 of them. `pair_flags`: A 1 at slot s joins slots s and s + 1 into one 2x2 block; no two 1s are adjacent and the last slot of a panel holds 0. `dest`: several delayed columns may share a slot. Of the 8 delayed columns held by one index of col, at most 2 go to pivot columns held by the same index of col. `linv`: each panel's matrix is unit lower triangular: ones on the diagonal, zeros above it.
All inputs are finite; a program needn't handle non-finite values.
Results may differ from a plain program's by a relative error of at most 0.00015.
Values sent between devices are 32-bit elements; how exact they have to be, the bound alone decides.
No kernel may reach another device: no remote copies, remote signals or barrier semaphores. Data moves between devices by JAX's collectives and lax.ppermute only.
A program may use at most 128 MiB of HBM per device.

v0:
```python
import jax
import jax.numpy as jnp
from jax import lax
from jax.experimental import pallas as pl
from jax.experimental.pallas import tpu as pltpu
from jax.sharding import PartitionSpec as P

AXES = ("row", "col")
ROWS, COLS = 8, 16
OWN = 64
DEL = 8
EXT = OWN + DEL
PAD = EXT + 8
PANEL = 256
PANELS = 4
SLOTS = PANEL * PANELS
LEAD = SLOTS - PANEL
KEXT = COLS * EXT
TILE = 256
F32, BF16 = jnp.float32, jnp.bfloat16
VMEM_BYTES = 56 * 1024 * 1024


def permute(value, pairs_of):
    pairs = []
    for r in range(ROWS):
        for c in range(COLS):
            to_r, to_c = pairs_of(r, c)
            pairs.append((r * COLS + c, to_r * COLS + to_c))
    return lax.ppermute(value, AXES, pairs)


def shift(value, y=0, core=0, z=0, x=0):
    return permute(
        value,
        lambda r, c: (
            (r // 2 + y) % 4 * 2 + (r % 2 + core) % 2,
            (c // 4 + z) % 4 * 4 + (c % 4 + x) % 4,
        ),
    )


def ring_small(value, axis):
    behind = shift(value, **{axis: 1})
    ahead = shift(value, **{axis: -1})
    across = shift(value, **{axis: 2})
    return jnp.concatenate([value, behind, across, ahead], axis=0)


def near_y(block):
    return shift(block, y=1), shift(block, y=-1)


def all_y(block, behind, ahead, core):
    relay = jnp.where(core == 0, behind, ahead)
    across = permute(relay, lambda r, c: ((r // 2 + (1 if r % 2 == 0 else -1)) % 4 * 2 + r % 2, c))
    return jnp.stack([block, behind, across, ahead], axis=0)


def mm(a, b, dims=((1,), (0,))):
    return lax.dot_general(a, b, (dims, ((), ())), preferred_element_type=F32)


def split(value):
    high = value.astype(BF16)
    return high, (value - high.astype(F32)).astype(BF16)


def mm3(a, b, dims=((1,), (0,))):
    return mm(a[0], b[0], dims) + mm(a[0], b[1], dims) + mm(a[1], b[0], dims)


def pick2(value, hot):
    high, low = split(value)
    return mm(high, hot) + mm(low, hot)


def hot(cond):
    return jnp.where(cond, 1.0, 0.0).astype(BF16)


def iota(shape, dim):
    return lax.broadcasted_iota(jnp.int32, shape, dim)


def extract_kernel(
    pivots_ref, dest_ref, delayed_ref, front_ref,
    piece_ref, crossing_ref, same_ref, other_ref, sorted_ref, slot_ref,
    front_buf, sems,
):
    rows_blk, width = front_buf.shape
    steps = rows_blk // TILE
    copies = []
    for i in range(steps):
        rows = pl.ds(i * TILE, TILE)
        copies.append(pltpu.make_async_copy(front_ref.at[rows, :], front_buf.at[rows, :], sems.at[i]))
        copies[-1].start()
    r, c = lax.axis_index("row"), lax.axis_index("col")

    value = pivots_ref[...].astype(F32)
    column = jnp.transpose(value)
    ranks = []
    for g in range(8):
        count = jnp.zeros((128, 128), F32)
        for h in range(8):
            count += jnp.where(value[h : h + 1, :] < column[:, g : g + 1], 1.0, 0.0)
        ranks.append(jnp.sum(count, axis=1, keepdims=True))
    lane = iota((128, 128), 1).astype(F32)
    sub = iota((128, 128), 0).astype(F32)
    for h in range(8):
        found = jnp.zeros((128, 128), F32)
        slot = jnp.zeros((128, 128), F32)
        for g in range(8):
            hit = ranks[g] == lane + 128.0 * h
            found += jnp.where(hit, column[:, g : g + 1], 0.0)
            slot += jnp.where(hit, sub + 128.0 * g, 0.0)
        sorted_ref[h : h + 1, :] = jnp.sum(found, axis=0, keepdims=True).astype(jnp.int32)
        slot_ref[h : h + 1, :] = jnp.sum(slot, axis=0, keepdims=True).astype(jnp.int32)

    own_cols = sorted_ref[pl.ds(c // 2, 1), :] - c * width
    own_rows = sorted_ref[pl.ds(r, 1), :] - r * rows_blk
    pick = hot(iota((width, 128), 0) == own_cols)
    total = jnp.zeros((EXT, 128), F32)
    for i in range(steps):
        copies[i].wait()
        rows = slice(i * TILE, (i + 1) * TILE)
        picked = jnp.transpose(pick2(front_buf[rows, :], pick))
        piece = jnp.concatenate([picked[:OWN] + picked[OWN:], delayed_ref[:, rows]], axis=0)
        piece_ref[:, rows] = piece
        total += pick2(piece, hot(iota((TILE, 128), 0) + i * TILE == own_rows))
    crossing_ref[:EXT, :] = total
    crossing_ref[EXT:, :] = jnp.zeros((PAD - EXT, 128), F32)
    crossing_ref[EXT : EXT + 1, :DEL] = dest_ref[...].astype(F32)

    @pl.when(c % 2 == 0)
    def _():
        same_ref[...] = piece_ref[:, :width]
        other_ref[...] = piece_ref[:, width:]

    @pl.when(c % 2 == 1)
    def _():
        same_ref[...] = piece_ref[:, width:]
        other_ref[...] = piece_ref[:, :width]


def order_kernel(slots_ref, crossing_ref, out_ref):
    count = crossing_ref.shape[0]
    high, low = split(crossing_ref[...])
    for p in range(PANELS - 1):
        rows = slice(p * PANEL, (p + 1) * PANEL)
        pick = hot(iota((PANEL, count), 0) + p * PANEL == slots_ref[...])
        out_ref[rows, :] = mm(pick, high) + mm(pick, low)


def weight_kernel(
    row_slots_ref, pi_slots_ref, mine_ref, mate_ref, linv_ref, diag_ref, next_ref, prev_ref,
    wh_ref, wl_ref, wide_ref,
    dh_ref, dl_ref,
):
    raw = jnp.concatenate([mine_ref[i] for i in range(4)] + [mate_ref[i] for i in range(4)], axis=1)
    raw_h, raw_l = split(raw)
    linv_t = [jnp.transpose(linv_ref[p]) for p in range(PANELS)]
    linv_s = [split(v) for v in linv_t]
    turned = jnp.transpose(row_slots_ref[...].astype(F32))
    row_slots = jnp.concatenate([turned[:, j : j + 1] for j in range(ROWS)], axis=0)
    turned = jnp.transpose(pi_slots_ref[...].astype(F32))
    pi_slots = jnp.concatenate([turned[:, j : j + 1] for j in range(COLS)], axis=0)
    cross = {}
    for p in range(1, PANELS):
        pick = hot(iota((SLOTS, PANEL), 1).astype(F32) + float(p * PANEL) == row_slots)
        rows = slice(0, p * PANEL)
        ordered = (mm(raw_h[rows], pick).astype(BF16), mm(raw_l[rows], pick).astype(BF16))
        product = mm3(ordered, linv_s[p])
        for q in range(p):
            cross[q, p] = split(product[q * PANEL : (q + 1) * PANEL])
    tables = {}
    w, wd = {}, {}
    for p in range(PANELS):
        lo = slice(p * PANEL, (p + 1) * PANEL)
        for s in range(p + 1):
            if s == p:
                value = linv_t[p]
            else:
                value = -sum(mm3(wd[s, q], tables[q, p]) for q in range(s, p))
            scaled = (
                value * diag_ref[:, lo]
                + pltpu.roll(value, PANEL - 1, 1) * next_ref[:, lo]
                + pltpu.roll(value, 1, 1) * prev_ref[:, lo]
            )
            w[s, p] = split(value)
            wd[s, p] = split(scaled)
            rows = slice(s * PANEL, (s + 1) * PANEL)
            wh_ref[rows, lo], wl_ref[rows, lo] = w[s, p]
            dh_ref[rows, lo], dl_ref[rows, lo] = wd[s, p]
        for n in range(p + 1, PANELS):
            tables[p, n] = split(sum(mm3(w[s, p], cross[s, n], ((0,), (0,))) for s in range(p + 1)))
    part = KEXT // 4
    for i in range(4):
        rows = slice(i * part, (i + 1) * part)
        low_rows = slice(KEXT + i * part, KEXT + (i + 1) * part)
        pick = hot(iota((part, SLOTS), 1).astype(F32) == pi_slots[rows])
        for p in range(PANELS):
            cols, depth = slice(p * PANEL, (p + 1) * PANEL), (p + 1) * PANEL
            wide_ref[rows, cols] = mm(pick[:, :depth], dh_ref[:depth, cols]).astype(BF16)
            wide_ref[low_rows, cols] = mm(pick[:, :depth], dl_ref[:depth, cols]).astype(BF16)


def scale_kernel(slots_ref, mine_ref, mate_ref, wh_ref, wl_ref, out_ref, ph_ref, pl_ref):
    got = jnp.concatenate([mine_ref[i] for i in range(4)] + [mate_ref[i] for i in range(4)], axis=0)
    got_h, got_l = split(got)
    for p in range(PANELS):
        rows = slice(p * PANEL, (p + 1) * PANEL)
        pick = hot(iota((PANEL, KEXT), 0) + p * PANEL == slots_ref[...])
        ph_ref[rows, :], pl_ref[rows, :] = split(mm(pick, got_h) + mm(pick, got_l))
    for p in range(PANELS):
        rows = slice(p * PANEL, (p + 1) * PANEL)
        deep = slice(0, (p + 1) * PANEL)
        total = mm3(
            (wh_ref[deep, rows], wl_ref[deep, rows]), (ph_ref[deep, :], pl_ref[deep, :]), ((0,), (0,))
        )
        out_ref[rows, :], out_ref[SLOTS + p * PANEL : SLOTS + (p + 1) * PANEL, :] = split(total)


def update_kernel(piece_ref, wide_ref, scaled_ref, front_ref, row_ref, col_ref, trailing_ref, factor_ref):
    high, low = split(piece_ref[...])
    high, low = jnp.transpose(high), jnp.transpose(low)
    factor = mm(jnp.concatenate([high, high], axis=1), wide_ref[...]) + mm(low, wide_ref[:KEXT, :])
    factor_ref[...] = factor
    high, low = split(factor)
    change = mm(jnp.concatenate([high, high], axis=1), scaled_ref[...]) + mm(low, scaled_ref[:SLOTS, :])
    keep = (row_ref[...] > 0.0) & (col_ref[...] > 0.0)
    trailing_ref[...] = jnp.where(keep, front_ref[...] - change, 0.0)


def whole(shape):
    return pl.BlockSpec(shape, lambda i: (0,) * len(shape), pipeline_mode=pl.Buffered(1))


PARAMS = pltpu.CompilerParams(vmem_limit_bytes=VMEM_BYTES)
VM = pl.BlockSpec(memory_space=pltpu.VMEM)
ANY = pl.BlockSpec(memory_space=pl.ANY)


def body(front, delayed, dest, pivots, pair_flags, linv, dinv_diag, dinv_off):
    rows_blk, cols_blk = front.shape
    r = lax.axis_index("row")
    c = lax.axis_index("col")
    y, core, z, x = r // 2, r % 2, c // 4, c % 4

    half = jax.ShapeDtypeStruct((EXT, cols_blk), F32)
    table = jax.ShapeDtypeStruct((8, 128), jnp.int32)
    piece, crossing, same, other, _, slot_at = pl.pallas_call(
        extract_kernel,
        in_specs=[VM, VM, VM, ANY],
        out_specs=[VM] * 6,
        out_shape=[
            jax.ShapeDtypeStruct((EXT, rows_blk), F32),
            jax.ShapeDtypeStruct((PAD, 2 * OWN), F32),
            half, half, table, table,
        ],
        scratch_shapes=[
            pltpu.VMEM((rows_blk, cols_blk), F32),
            pltpu.SemaphoreType.DMA((rows_blk // TILE,)),
        ],
        compiler_params=PARAMS,
        name="extract",
    )(pivots.reshape(8, 128), dest[None, :], delayed, front)

    crossing = ring_small(ring_small(crossing, "x"), "z")
    crossing, piece, same, other = lax.optimization_barrier((crossing, piece, same, other))

    gathered = lax.all_gather(piece, "col", axis=0, tiled=True)

    dest_rel = crossing.reshape(COLS, PAD, 2 * OWN)[:, EXT, :DEL].astype(jnp.int32)
    rel = jnp.arange(COLS, dtype=jnp.int32)
    source = (z - rel // 4) % 4 * 4 + (x - rel % 4) % 4
    slot_table = slot_at.reshape(COLS, OWN)
    cross_slots = jnp.concatenate(
        [slot_table[source], dest_rel, jnp.full((COLS, PAD - EXT), -1, jnp.int32)], axis=1
    ).reshape(1, COLS * PAD)
    ext = jnp.concatenate([slot_table, dest_rel[source]], axis=1)
    ordered = pl.pallas_call(
        order_kernel,
        out_shape=jax.ShapeDtypeStruct((LEAD, 2 * OWN), F32),
        compiler_params=PARAMS,
        name="order",
    )(cross_slots, crossing)
    near = near_y(ordered)

    parity = c % 2
    sent = [
        permute(
            value,
            lambda a, b, flip=flip: (
                (b // 4 + a // 2) % 4 * 2 + b % 4 // 2,
                2 * a + ((b % 2) ^ flip),
            ),
        )
        for flip, value in enumerate((same, other))
    ]

    rel_row = jnp.arange(ROWS, dtype=jnp.int32)
    row_source = (y - rel_row % 4) % 4 * 2 + (core + rel_row // 4) % 2
    row_slots = slot_at[row_source]
    coupled = pair_flags.astype(F32) * dinv_off
    coupled_prev = jnp.concatenate([jnp.zeros_like(coupled[:1]), coupled[:-1]])
    first = (row_source // 2 - z) % 4 * 4 + row_source % 2 * 2
    pair = jnp.stack([first + parity, first + 1 - parity], axis=1).reshape(COLS)
    pair_slots = ext[pair].reshape(1, KEXT)
    row_ids = r * rows_blk + jnp.arange(rows_blk, dtype=jnp.int32)
    col_ids = c * cols_blk + jnp.arange(cols_blk, dtype=jnp.int32)
    row_keep = 1.0 - jnp.any(row_ids[:, None] == pivots[None, :], axis=1).astype(F32)[:, None]
    col_keep = 1.0 - jnp.any(col_ids[:, None] == pivots[None, :], axis=1).astype(F32)[None, :]
    small = (row_slots, ext, pair_slots, row_keep, col_keep, coupled, coupled_prev)
    near, small = lax.optimization_barrier((near, small))
    row_slots, ext, pair_slots, row_keep, col_keep, coupled, coupled_prev = small

    ordered_mine = all_y(ordered, *near, core)
    strip = jnp.concatenate(sent, axis=0)
    ordered_mine, strip = lax.optimization_barrier((ordered_mine, strip))
    ordered_mate = shift(ordered_mine, core=1)
    near = near_y(strip)
    square = jax.ShapeDtypeStruct((SLOTS, SLOTS), BF16)
    weights = pl.pallas_call(
        weight_kernel,
        out_shape=[square, square, jax.ShapeDtypeStruct((2 * KEXT, SLOTS), BF16)],
        scratch_shapes=[pltpu.VMEM((SLOTS, SLOTS), BF16)] * 2,
        compiler_params=PARAMS,
        name="weights",
    )(
        row_slots, ext, ordered_mine, ordered_mate, linv,
        dinv_diag[None, :], coupled[None, :], coupled_prev[None, :],
    )
    near, (w_high, w_low, wide) = lax.optimization_barrier((near, weights))
    strip_mine = all_y(strip, *near, core)
    strip_mate = shift(strip_mine, core=1)
    scaled = pl.pallas_call(
        scale_kernel,
        out_shape=jax.ShapeDtypeStruct((2 * SLOTS, cols_blk), BF16),
        scratch_shapes=[pltpu.VMEM((SLOTS, cols_blk), BF16)] * 2,
        compiler_params=PARAMS,
        name="scale",
    )(pair_slots, strip_mine, strip_mate, w_high, w_low)

    tile = 2 * TILE
    trailing, factor = pl.pallas_call(
        update_kernel,
        grid=(rows_blk // tile,),
        in_specs=[
            pl.BlockSpec((KEXT, tile), lambda i: (0, i)),
            whole((2 * KEXT, SLOTS)),
            whole((2 * SLOTS, cols_blk)),
            pl.BlockSpec((tile, cols_blk), lambda i: (i, 0)),
            pl.BlockSpec((tile, 1), lambda i: (i, 0)),
            whole((1, cols_blk)),
        ],
        out_specs=[
            pl.BlockSpec((tile, cols_blk), lambda i: (i, 0)),
            pl.BlockSpec((tile, SLOTS), lambda i: (i, 0)),
        ],
        out_shape=[
            jax.ShapeDtypeStruct((rows_blk, cols_blk), F32),
            jax.ShapeDtypeStruct((rows_blk, SLOTS), F32),
        ],
        compiler_params=PARAMS,
        name="update",
    )(gathered, wide, scaled, front, row_keep, col_keep)
    return (trailing, factor)


def solution(mesh):
    return jax.shard_map(
        body,
        mesh=mesh,
        in_specs=(P("row", "col"), P("col", "row"), P("col"), P(), P(), P(), P(), P()),
        out_specs=(P("row", "col"), P("row", None)),
        check_vma=False,
    )
```

profile of v0, /device:TPU:97, one launch (start us, length us, event | category | flops | bytes accessed | tf_op | source)
XLA Modules:
  0.0 156.2 jit_solution(8416072117812594077)
XLA Ops:
  7.2 6.9 %extract.1 = (f32[72,1536]{1,0:T(8,128)}, f32[80,128]{1,0:T(8,128)}, f32[72,768]{1,0:T(8,128)}, f32[72,768]{1,0:T(8,128)}, s32[8,128]{1,0:T(8,128)}, /*index=5*/s32[8,128]{1,0:T(8,128)}) custom-call(s32[8,128]{1,0:T(8,128)} %bitcast.32, s32[1,8]{1,0:T(1,128)} %bitcast.37, f32[8,1536]{1,0:T(8,128)} %delayed_ref.1, f32[1536,768]{1,0:T(8,128)} %front_ref.3), custom_call_target="tpu_custom_call" | custom-call | tf_op jit(solution)/shard_map/extract/pallas_call | solution.py:252
  14.2 2.6 %collective-permute-start.2 = (f32[80,128]{1,0:T(8,128)}, f32[80,128]{1,0:T(8,128)S(1)}, u32[]{:S(2)}, u32[]{:S(2)}) collective-permute-start(f32[80,128]{1,0:T(8,128)} %get-tuple-element.30), channel_id=1, source_target_pairs={{0,3},{1,0},{2,1},{3,2},{4,7},{5,4},{6,5},{7,6},{8,11},{9,8},{10,9... | collective-permute-start | bytes 122888 | tf_op jit(solution)/shard_map/ppermute | solution.py:30
  16.8 0.5 collective-permute-start.1
  17.3 0.6 collective-permute-start
  17.9 0.8 constant_dynamic-update-slice_fusion.3
  18.7 3.1 %collective-permute-done = f32[80,128]{1,0:T(8,128)S(1)} collective-permute-done((f32[80,128]{1,0:T(8,128)}, f32[80,128]{1,0:T(8,128)S(1)}, u32[]{:S(2)}, u32[]{:S(2)}) %collective-permute-start) | collective-permute-done | bytes 40992 | tf_op jit(solution)/shard_map/ppermute | solution.py:30
  21.9 1.9 %collective-permute-start.4 = (f32[320,128]{1,0:T(8,128)S(1)}, f32[320,128]{1,0:T(8,128)S(1)}, u32[]{:S(2)}, u32[]{:S(2)}) collective-permute-start(f32[320,128]{1,0:T(8,128)S(1)} %get-tuple-element.58), channel_id=1, source_target_pairs={{0,8},{1,9},{2,10},{3,11},{4,12},{5,13},{6,14},{7,15},{8,0},{9,1},... | collective-permute-start | bytes 491528 | tf_op jit(solution)/shard_map/ppermute | solution.py:30
  23.8 2.3 %collective-permute-done.3 = f32[320,128]{1,0:T(8,128)S(1)} collective-permute-done((f32[320,128]{1,0:T(8,128)S(1)}, f32[320,128]{1,0:T(8,128)S(1)}, u32[]{:S(2)}, u32[]{:S(2)}) %collective-permute-start.3) | collective-permute-done | bytes 163872 | tf_op jit(solution)/shard_map/ppermute | solution.py:30
  26.1 1.6 %collective-permute-done.4 = f32[320,128]{1,0:T(8,128)S(1)} collective-permute-done((f32[320,128]{1,0:T(8,128)S(1)}, f32[320,128]{1,0:T(8,128)S(1)}, u32[]{:S(2)}, u32[]{:S(2)}) %collective-permute-start.4) | collective-permute-done | bytes 163872 | tf_op jit(solution)/shard_map/ppermute | solution.py:30
  27.7 2.9 %collective-permute-done.5 = f32[320,128]{1,0:T(8,128)S(1)} collective-permute-done((f32[320,128]{1,0:T(8,128)S(1)}, f32[320,128]{1,0:T(8,128)S(1)}, u32[]{:S(2)}, u32[]{:S(2)}) %collective-permute-start.5) | collective-permute-done | bytes 163872 | tf_op jit(solution)/shard_map/ppermute | solution.py:30
  30.8 0.1 pad.18.clone
  30.9 0.1 copy.25
  31.0 0.1 reshape.481
  31.1 0.5 compare_reduce_fusion.1
  31.6 0.6 sub.146.col_ref
  32.2 1.0 compare_reduce_fusion
  33.3 1.1 gather_fusion.1
  34.5 0.6 gather_fusion
  35.1 0.1 copy.23
  35.2 0.1 add_add_fusion
  35.3 0.7 reshape.480.slots_ref
  36.0 3.1 %order.1 = f32[768,128]{1,0:T(8,128)} custom-call(s32[1,1280]{1,0:T(1,128)} %reshape.480.slots_ref, f32[1280,128]{1,0:T(8,128)} %copy-done.6), custom_call_target="tpu_custom_call" | custom-call | tf_op jit(solution)/shard_map/order/pallas_call | solution.py:282
  39.0 2.7 %collective-permute-start.7 = (f32[768,128]{1,0:T(8,128)}, f32[768,128]{1,0:T(8,128)S(1)}, u32[]{:S(2)}, u32[]{:S(2)}) collective-permute-start(f32[768,128]{1,0:T(8,128)} %order.1), channel_id=1, source_target_pairs={{0,96},{1,97},{2,98},{3,99},{4,100},{5,101},{6,102},{7,103},{8,104... | collective-permute-start | bytes 1179656 | tf_op jit(solution)/shard_map/ppermute | solution.py:30
  41.8 0.7 pad_maximum_fusion.3
  42.5 0.6 gather_fusion.2
  43.0 0.1 pad_add_fusion.pi_slots_ref
  43.1 0.6 gather_fusion.3
  43.7 0.7 reshape.482.slots_ref
  44.3 3.0 %collective-permute-done.7 = f32[768,128]{1,0:T(8,128)S(1)} collective-permute-done((f32[768,128]{1,0:T(8,128)}, f32[768,128]{1,0:T(8,128)S(1)}, u32[]{:S(2)}, u32[]{:S(2)}) %collective-permute-start.7) | collective-permute-done | bytes 393248 | tf_op jit(solution)/shard_map/ppermute | solution.py:30
  47.4 3.0 %collective-permute-done.6 = f32[768,128]{1,0:T(8,128)S(1)} collective-permute-done((f32[768,128]{1,0:T(8,128)}, f32[768,128]{1,0:T(8,128)S(1)}, u32[]{:S(2)}, u32[]{:S(2)}) %collective-permute-start.6) | collective-permute-done | bytes 393248 | tf_op jit(solution)/shard_map/ppermute | solution.py:30
  50.4 0.5 collective-permute-start.8
  50.9 9.6 %collective-permute-start.9 = (f32[72,768]{1,0:T(8,128)S(1)}, f32[72,768]{1,0:T(8,128)S(1)}, u32[]{:S(2)}, u32[]{:S(2)}) collective-permute-start(f32[72,768]{1,0:T(8,128)S(1)} %copy-done.13), channel_id=1, source_target_pairs={{0,0},{1,1},{2,16},{3,17},{4,32},{5,33},{6,48},{7,49},{8,64},{9,65... | collective-permute-start | bytes 663560 | tf_op jit(solution)/shard_map/ppermute | solution.py:30
  60.6 5.6 %collective-permute-done.9 = f32[72,768]{1,0:T(8,128)S(1)} collective-permute-done((f32[72,768]{1,0:T(8,128)S(1)}, f32[72,768]{1,0:T(8,128)S(1)}, u32[]{:S(2)}, u32[]{:S(2)}) %collective-permute-start.9) | collective-permute-done | bytes 221216 | tf_op jit(solution)/shard_map/ppermute | solution.py:30
  66.2 6.5 %collective-permute-done.10 = f32[72,768]{1,0:T(8,128)S(1)} collective-permute-done((f32[72,768]{1,0:T(8,128)S(1)}, f32[72,768]{1,0:T(8,128)S(1)}, u32[]{:S(2)}, u32[]{:S(2)}) %collective-permute-start.10) | collective-permute-done | bytes 221216 | tf_op jit(solution)/shard_map/ppermute | solution.py:30
  72.8 0.1 pad_maximum_fusion.1.mine_ref
  72.9 3.3 %collective-permute-start.13 = (f32[4,768,128]{2,1,0:T(8,128)S(1)}, f32[4,768,128]{2,1,0:T(8,128)S(1)}, u32[]{:S(2)}, u32[]{:S(2)}) collective-permute-start(f32[4,768,128]{2,1,0:T(8,128)S(1)} %pad_maximum_fusion.1.mine_ref), channel_id=1, source_target_pairs={{0,16},{1,17},{2,18},{3,19},{4,20},{5,21},{6,22},{7,23},{8,24},{9,... | collective-permute-start | bytes 4718600 | tf_op jit(solution)/shard_map/ppermute | solution.py:30
  76.2 1.5 collective-permute-start.11
  77.7 1.6 %collective-permute-done.13.mate_ref = f32[4,768,128]{2,1,0:T(8,128)S(1)} collective-permute-done((f32[4,768,128]{2,1,0:T(8,128)S(1)}, f32[4,768,128]{2,1,0:T(8,128)S(1)}, u32[]{:S(2)}, u32[]{:S(2)}) %collective-permute-start.13) | collective-permute-done | bytes 1572896 | tf_op jit(solution)/shard_map/ppermute | solution.py:30
  79.3 1.1 copy-done.4
  80.4 13.2 %weights.1 = (bf16[1024,1024]{1,0:T(8,128)(2,1)}, bf16[1024,1024]{1,0:T(8,128)(2,1)}, bf16[2304,1024]{1,0:T(8,128)(2,1)}) custom-call(s32[8,128]{1,0:T(8,128)} %gather_fusion.1, s32[16,72]{1,0:T(8,128)} %copy-done.5, f32[4,768,128]{2,1,0:T(8,128)} %copy-done.1, f32[4,768,128]{2,1,0:T(8,128)} %copy-done.4, f32[4,256,256]{2,1,0:T(8,128)} %linv_ref.1, ...), custom_call_target="tpu_custom_call" | custom-call | tf_op jit(solution)/shard_map/weights/pallas_call | solution.py:324
  93.8 7.5 %collective-permute-done.14 = f32[144,768]{1,0:T(8,128)S(1)} collective-permute-done((f32[144,768]{1,0:T(8,128)S(1)}, f32[144,768]{1,0:T(8,128)S(1)}, u32[]{:S(2)}, u32[]{:S(2)}) %collective-permute-start.14) | collective-permute-done | bytes 442400 | tf_op jit(solution)/shard_map/ppermute | solution.py:30
  101.3 0.1 pad_maximum_fusion.mine_ref
  101.5 2.6 %collective-permute-start.15 = (f32[4,144,768]{2,1,0:T(8,128)S(1)}, f32[4,144,768]{2,1,0:T(8,128)S(1)}, u32[]{:S(2)}, u32[]{:S(2)}) collective-permute-start(f32[4,144,768]{2,1,0:T(8,128)S(1)} %pad_maximum_fusion.mine_ref), channel_id=1, source_target_pairs={{0,16},{1,17},{2,18},{3,19},{4,20},{5,21},{6,22},{7,23},{8,24},{9,... | collective-permute-start | bytes 5308424 | tf_op jit(solution)/shard_map/ppermute | solution.py:30
  104.1 1.2 copy.26.row_ref
  105.3 2.1 %collective-permute-done.15.mate_ref = f32[4,144,768]{2,1,0:T(8,128)S(1)} collective-permute-done((f32[4,144,768]{2,1,0:T(8,128)S(1)}, f32[4,144,768]{2,1,0:T(8,128)S(1)}, u32[]{:S(2)}, u32[]{:S(2)}) %collective-permute-start.15) | collective-permute-done | bytes 1769504 | tf_op jit(solution)/shard_map/ppermute | solution.py:30
  107.4 1.2 copy-done.2
  108.7 12.3 %scale.1.scaled_ref = bf16[2048,768]{1,0:T(8,128)(2,1)} custom-call(s32[1,1152]{1,0:T(1,128)} %reshape.482.slots_ref, f32[4,144,768]{2,1,0:T(8,128)} %copy-done, f32[4,144,768]{2,1,0:T(8,128)} %copy-done.2, bf16[1024,1024]{1,0:T(8,128)(2,1)} %get-tuple-element.54.wh_ref, bf16[1024,1024]{1,0:T(8,128)(2,1)} %get-tuple-element.55.wl_ref), custom_call_target="tpu_custom_call" | custom-call | tf_op jit(solution)/shard_map/scale/pallas_call | solution.py:337
  121.0 28.3 %update.1 = (f32[1536,768]{1,0:T(8,128)}, f32[1536,1024]{1,0:T(8,128)}) custom-call(f32[1152,1536]{1,0:T(8,128)} %all-gather.2.cloned.1.call-done.piece_ref, bf16[2304,1024]{1,0:T(8,128)(2,1)} %get-tuple-element.50.wide_ref, bf16[2048,768]{1,0:T(8,128)(2,1)} %scale.1.scaled_ref, f32[1536,768]{1,0:T(8,128)} %front_ref.3, f32[1536,1]{1,0:T(8,128)} %copy.26.row_ref, ...), custom_call_target="tpu_custom_call" | custom-call | tf_op jit(solution)/shard_map/update/pallas_call | solution.py:346
  (68 shorter events, 0.8 us)
Async XLA Ops:
  7.2 113.9 %all-gather.2.cloned.1.call-start = ((), (), s32[]{:S(2)}) async-start(), calls=%async_computation | async-start | bytes 7520256 | tf_op jit(solution)/shard_map/all_gather | solution.py:272
  14.1 16.9 %copy-start.8 = (s32[1024]{0:T(1024)S(1)}, s32[1024]{0:T(1024)}, u32[]{:S(2)}) copy-start(s32[1024]{0:T(1024)} %param.11) | copy-start | bytes 12292
  14.2 19.0 %copy-start.7 = (s32[8,128]{1,0:T(8,128)S(1)}, s32[8,128]{1,0:T(8,128)}, u32[]{:S(2)}) copy-start(s32[8,128]{1,0:T(8,128)} %get-tuple-element.35) | copy-start | bytes 12292
  14.2 27.6 %copy-start.10 = (f32[1024]{0:T(1024)S(1)}, f32[1024]{0:T(1024)}, u32[]{:S(2)}) copy-start(f32[1024]{0:T(1024)} %param.15) | copy-start | bytes 12292
  14.2 27.6 %copy-start.11 = (s32[1024]{0:T(1024)S(1)}, s32[1024]{0:T(1024)}, u32[]{:S(2)}) copy-start(s32[1024]{0:T(1024)} %param.12) | copy-start | bytes 12292
  14.2 7.6 %collective-permute-start.2 = (f32[80,128]{1,0:T(8,128)}, f32[80,128]{1,0:T(8,128)S(1)}, u32[]{:S(2)}, u32[]{:S(2)}) collective-permute-start(f32[80,128]{1,0:T(8,128)} %get-tuple-element.30), channel_id=1, source_target_pairs={{0,3},{1,0},{2,1},{3,2},{4,7},{5,4},{6,5},{7,6},{8,11},{9,8},{10,9... | collective-permute-start | bytes 122888 | tf_op jit(solution)/shard_map/ppermute | solution.py:30
  16.8 5.0 %collective-permute-start.1 = (f32[80,128]{1,0:T(8,128)}, f32[80,128]{1,0:T(8,128)S(1)}, u32[]{:S(2)}, u32[]{:S(2)}) collective-permute-start(f32[80,128]{1,0:T(8,128)} %get-tuple-element.30), channel_id=1, source_target_pairs={{0,2},{1,3},{2,0},{3,1},{4,6},{5,7},{6,4},{7,5},{8,10},{9,11},{10,... | collective-permute-start | bytes 122888 | tf_op jit(solution)/shard_map/ppermute | solution.py:30
  17.3 4.5 %collective-permute-start = (f32[80,128]{1,0:T(8,128)}, f32[80,128]{1,0:T(8,128)S(1)}, u32[]{:S(2)}, u32[]{:S(2)}) collective-permute-start(f32[80,128]{1,0:T(8,128)} %get-tuple-element.30), channel_id=1, source_target_pairs={{0,1},{1,2},{2,3},{3,0},{4,5},{5,6},{6,7},{7,4},{8,9},{9,10},{10,1... | collective-permute-start | bytes 122888 | tf_op jit(solution)/shard_map/ppermute | solution.py:30
  21.8 4.2 %collective-permute-start.3 = (f32[320,128]{1,0:T(8,128)S(1)}, f32[320,128]{1,0:T(8,128)S(1)}, u32[]{:S(2)}, u32[]{:S(2)}) collective-permute-start(f32[320,128]{1,0:T(8,128)S(1)} %get-tuple-element.58), channel_id=1, source_target_pairs={{0,4},{1,5},{2,6},{3,7},{4,8},{5,9},{6,10},{7,11},{8,12},{9,13},{1... | collective-permute-start | bytes 491528 | tf_op jit(solution)/shard_map/ppermute | solution.py:30
  21.9 5.8 %collective-permute-start.4 = (f32[320,128]{1,0:T(8,128)S(1)}, f32[320,128]{1,0:T(8,128)S(1)}, u32[]{:S(2)}, u32[]{:S(2)}) collective-permute-start(f32[320,128]{1,0:T(8,128)S(1)} %get-tuple-element.58), channel_id=1, source_target_pairs={{0,8},{1,9},{2,10},{3,11},{4,12},{5,13},{6,14},{7,15},{8,0},{9,1},... | collective-permute-start | bytes 491528 | tf_op jit(solution)/shard_map/ppermute | solution.py:30
  23.8 6.9 %collective-permute-start.5 = (f32[320,128]{1,0:T(8,128)S(1)}, f32[320,128]{1,0:T(8,128)S(1)}, u32[]{:S(2)}, u32[]{:S(2)}) collective-permute-start(f32[320,128]{1,0:T(8,128)S(1)} %get-tuple-element.58), channel_id=1, source_target_pairs={{0,12},{1,13},{2,14},{3,15},{4,0},{5,1},{6,2},{7,3},{8,4},{9,5},{1... | collective-permute-start | bytes 491528 | tf_op jit(solution)/shard_map/ppermute | solution.py:30
  27.7 23.2 %copy-start.13 = (f32[72,768]{1,0:T(8,128)S(1)}, f32[72,768]{1,0:T(8,128)}, u32[]{:S(2)}) copy-start(f32[72,768]{1,0:T(8,128)} %get-tuple-element.39) | copy-start | bytes 663556
  27.7 32.8 %copy-start.12 = (f32[72,768]{1,0:T(8,128)S(1)}, f32[72,768]{1,0:T(8,128)}, u32[]{:S(2)}) copy-start(f32[72,768]{1,0:T(8,128)} %get-tuple-element.40) | copy-start | bytes 663556
  30.7 5.3 %copy-start.6 = (f32[1280,128]{1,0:T(8,128)}, f32[1280,128]{1,0:T(8,128)S(1)}, u32[]{:S(2)}) copy-start(f32[1280,128]{1,0:T(8,128)S(1)} %constant_dynamic-update-slice_fusion.4.crossing_ref) | copy-start | bytes 1966084
  39.0 33.7 %copy-start.3 = (f32[768,128]{1,0:T(8,128)S(1)}, f32[768,128]{1,0:T(8,128)}, u32[]{:S(2)}) copy-start(f32[768,128]{1,0:T(8,128)} %order.1) | copy-start | bytes 1179652
  39.0 8.3 %collective-permute-start.7 = (f32[768,128]{1,0:T(8,128)}, f32[768,128]{1,0:T(8,128)S(1)}, u32[]{:S(2)}, u32[]{:S(2)}) collective-permute-start(f32[768,128]{1,0:T(8,128)} %order.1), channel_id=1, source_target_pairs={{0,96},{1,97},{2,98},{3,99},{4,100},{5,101},{6,102},{7,103},{8,104... | collective-permute-start | bytes 1179656 | tf_op jit(solution)/shard_map/ppermute | solution.py:30
  41.8 8.6 %collective-permute-start.6 = (f32[768,128]{1,0:T(8,128)}, f32[768,128]{1,0:T(8,128)S(1)}, u32[]{:S(2)}, u32[]{:S(2)}) collective-permute-start(f32[768,128]{1,0:T(8,128)} %order.1), channel_id=1, source_target_pairs={{0,32},{1,33},{2,34},{3,35},{4,36},{5,37},{6,38},{7,39},{8,40},{9,... | collective-permute-start | bytes 1179656 | tf_op jit(solution)/shard_map/ppermute | solution.py:30
  41.8 31.1 %copy-start.9 = (f32[1024]{0:T(1024)}, f32[1024]{0:T(1024)S(1)}, u32[]{:S(2)}) copy-start(f32[1024]{0:T(1024)S(1)} %convert_multiply_fusion) | copy-start | bytes 12292
  43.1 29.8 %copy-start.5 = (s32[16,72]{1,0:T(8,128)}, s32[16,72]{1,0:T(8,128)S(1)}, u32[]{:S(2)}) copy-start(s32[16,72]{1,0:T(8,128)S(1)} %pad_add_fusion.pi_slots_ref) | copy-start | bytes 13828
  50.4 22.3 %collective-permute-start.8 = (f32[768,128]{1,0:T(8,128)S(1)}, f32[768,128]{1,0:T(8,128)S(1)}, u32[]{:S(2)}, u32[]{:S(2)}) collective-permute-start(f32[768,128]{1,0:T(8,128)S(1)} %broadcast_select_fusion.1), channel_id=1, source_target_pairs={{0,32},{1,33},{2,34},{3,35},{4,36},{5,37},{6,38},{7,39},{8,40},{9,... | collective-permute-start | bytes 1179656 | tf_op jit(solution)/shard_map/ppermute | solution.py:30
  50.9 15.3 %collective-permute-start.9 = (f32[72,768]{1,0:T(8,128)S(1)}, f32[72,768]{1,0:T(8,128)S(1)}, u32[]{:S(2)}, u32[]{:S(2)}) collective-permute-start(f32[72,768]{1,0:T(8,128)S(1)} %copy-done.13), channel_id=1, source_target_pairs={{0,0},{1,1},{2,16},{3,17},{4,32},{5,33},{6,48},{7,49},{8,64},{9,65... | collective-permute-start | bytes 663560 | tf_op jit(solution)/shard_map/ppermute | solution.py:30
  60.5 12.2 %collective-permute-start.10 = (f32[72,768]{1,0:T(8,128)S(1)}, f32[72,768]{1,0:T(8,128)S(1)}, u32[]{:S(2)}, u32[]{:S(2)}) collective-permute-start(f32[72,768]{1,0:T(8,128)S(1)} %copy-done.12), channel_id=1, source_target_pairs={{0,1},{1,0},{2,17},{3,16},{4,33},{5,32},{6,49},{7,48},{8,65},{9,64... | collective-permute-start | bytes 663560 | tf_op jit(solution)/shard_map/ppermute | solution.py:30
  72.9 6.3 %copy-start.1 = (f32[4,768,128]{2,1,0:T(8,128)}, f32[4,768,128]{2,1,0:T(8,128)S(1)}, u32[]{:S(2)}) copy-start(f32[4,768,128]{2,1,0:T(8,128)S(1)} %pad_maximum_fusion.1.mine_ref) | copy-start | bytes 4718596
  72.9 6.3 %collective-permute-start.13 = (f32[4,768,128]{2,1,0:T(8,128)S(1)}, f32[4,768,128]{2,1,0:T(8,128)S(1)}, u32[]{:S(2)}, u32[]{:S(2)}) collective-permute-start(f32[4,768,128]{2,1,0:T(8,128)S(1)} %pad_maximum_fusion.1.mine_ref), channel_id=1, source_target_pairs={{0,16},{1,17},{2,18},{3,19},{4,20},{5,21},{6,22},{7,23},{8,24},{9,... | collective-permute-start | bytes 4718600 | tf_op jit(solution)/shard_map/ppermute | solution.py:30
  76.2 17.4 %collective-permute-start.12 = (f32[144,768]{1,0:T(8,128)S(1)}, f32[144,768]{1,0:T(8,128)S(1)}, u32[]{:S(2)}, u32[]{:S(2)}) collective-permute-start(f32[144,768]{1,0:T(8,128)S(1)} %pad_maximum_fusion.2), channel_id=1, source_target_pairs={{0,96},{1,97},{2,98},{3,99},{4,100},{5,101},{6,102},{7,103},{8,104... | collective-permute-start | bytes 1327112 | tf_op jit(solution)/shard_map/ppermute | solution.py:30
  76.2 17.4 %collective-permute-start.11 = (f32[144,768]{1,0:T(8,128)S(1)}, f32[144,768]{1,0:T(8,128)S(1)}, u32[]{:S(2)}, u32[]{:S(2)}) collective-permute-start(f32[144,768]{1,0:T(8,128)S(1)} %pad_maximum_fusion.2), channel_id=1, source_target_pairs={{0,32},{1,33},{2,34},{3,35},{4,36},{5,37},{6,38},{7,39},{8,40},{9,... | collective-permute-start | bytes 1327112 | tf_op jit(solution)/shard_map/ppermute | solution.py:30
  79.3 1.1 copy-start.4
  93.7 7.6 %collective-permute-start.14 = (f32[144,768]{1,0:T(8,128)S(1)}, f32[144,768]{1,0:T(8,128)S(1)}, u32[]{:S(2)}, u32[]{:S(2)}) collective-permute-start(f32[144,768]{1,0:T(8,128)S(1)} %broadcast_select_fusion), channel_id=1, source_target_pairs={{0,32},{1,33},{2,34},{3,35},{4,36},{5,37},{6,38},{7,39},{8,40},{9,... | collective-permute-start | bytes 1327112 | tf_op jit(solution)/shard_map/ppermute | solution.py:30
  101.5 6.0 %copy-start = (f32[4,144,768]{2,1,0:T(8,128)}, f32[4,144,768]{2,1,0:T(8,128)S(1)}, u32[]{:S(2)}) copy-start(f32[4,144,768]{2,1,0:T(8,128)S(1)} %pad_maximum_fusion.mine_ref) | copy-start | bytes 5308420
  101.5 5.9 %collective-permute-start.15 = (f32[4,144,768]{2,1,0:T(8,128)S(1)}, f32[4,144,768]{2,1,0:T(8,128)S(1)}, u32[]{:S(2)}, u32[]{:S(2)}) collective-permute-start(f32[4,144,768]{2,1,0:T(8,128)S(1)} %pad_maximum_fusion.mine_ref), channel_id=1, source_target_pairs={{0,16},{1,17},{2,18},{3,19},{4,20},{5,21},{6,22},{7,23},{8,24},{9,... | collective-permute-start | bytes 5308424 | tf_op jit(solution)/shard_map/ppermute | solution.py:30
  107.4 1.2 copy-start.2
Sparse Core Ops, SparseCore 0:
  30.8 74.1 all-gather.1
where the time goes:
time: 156 us
  Pallas kernels  63.9 us (41%)
  waiting for transfers between devices  39.3 us (25%)
  starting transfers between devices  26 us (17%)
  between operations  14.4 us (9%)
  local copies, waits for them, and re-layouts  9.75 us (6%)
  other arithmetic  2.83 us (2%)
    ppermute x16, waiting for transfers between devices, permute(): return lax.ppermute(value, AXES, pairs)  39.3 us
    pallas_call x1, Pallas kernels, body(): pl.pallas_call(update_kernel, grid=(rows_blk // tile,), in_specs=[pl.Bloc...  28.3 us
    ppermute x16, starting transfers between devices, permute(): return lax.ppermute(value, AXES, pairs)  26 us
    pallas_call x1, Pallas kernels, body(): pl.pallas_call(weight_kernel, out_shape=[square, square, jax.ShapeDtypeSt...  13.2 us
    pallas_call x1, Pallas kernels, body(): pl.pallas_call(scale_kernel, out_shape=jax.ShapeDtypeStruct((2 * SLOTS, c...  12.3 us
    pallas_call x1, Pallas kernels, body(): pl.pallas_call(extract_kernel, in_specs=[VM, VM, VM, ANY], out_specs=[VM]...  6.93 us
    unnamed x34, local copies, waits for them, and re-layouts  3.36 us
  transfers between devices with their start and end apart: 17, of which 11 were waited for; matrix products, arithmetic and copies ran while one was open for 6% of the time, Pallas kernels for 18%

commit v1 on v0

--- a/solution.py
+++ b/solution.py
@@ -153,9 +153,8 @@
 
 
 def weight_kernel(
-    row_slots_ref, pi_slots_ref, mine_ref, mate_ref, linv_ref, diag_ref, next_ref, prev_ref,
-    wh_ref, wl_ref, wide_ref,
-    dh_ref, dl_ref,
+    row_slots_ref, mine_ref, mate_ref, linv_ref, diag_ref, next_ref, prev_ref,
+    wh_ref, wl_ref, dh_ref, dl_ref,
 ):
     raw = jnp.concatenate([mine_ref[i] for i in range(4)] + [mate_ref[i] for i in range(4)], axis=1)
     raw_h, raw_l = split(raw)
@@ -163,8 +162,6 @@
     linv_s = [split(v) for v in linv_t]
     turned = jnp.transpose(row_slots_ref[...].astype(F32))
     row_slots = jnp.concatenate([turned[:, j : j + 1] for j in range(ROWS)], axis=0)
-    turned = jnp.transpose(pi_slots_ref[...].astype(F32))
-    pi_slots = jnp.concatenate([turned[:, j : j + 1] for j in range(COLS)], axis=0)
     cross = {}
     for p in range(1, PANELS):
         pick = hot(iota((SLOTS, PANEL), 1).astype(F32) + float(p * PANEL) == row_slots)
@@ -194,6 +191,11 @@
             dh_ref[rows, lo], dl_ref[rows, lo] = wd[s, p]
         for n in range(p + 1, PANELS):
             tables[p, n] = split(sum(mm3(w[s, p], cross[s, n], ((0,), (0,))) for s in range(p + 1)))
+
+
+def expand_kernel(pi_slots_ref, dh_ref, dl_ref, wide_ref):
+    turned = jnp.transpose(pi_slots_ref[...].astype(F32))
+    pi_slots = jnp.concatenate([turned[:, j : j + 1] for j in range(COLS)], axis=0)
     part = KEXT // 4
     for i in range(4):
         rows = slice(i * part, (i + 1) * part)
@@ -285,6 +287,7 @@
         compiler_params=PARAMS,
         name="order",
     )(cross_slots, crossing)
+    ordered, pivots, slot_at = lax.optimization_barrier((ordered, pivots, slot_at))
     near = near_y(ordered)
 
     parity = c % 2
@@ -323,16 +326,22 @@
     square = jax.ShapeDtypeStruct((SLOTS, SLOTS), BF16)
     weights = pl.pallas_call(
         weight_kernel,
-        out_shape=[square, square, jax.ShapeDtypeStruct((2 * KEXT, SLOTS), BF16)],
-        scratch_shapes=[pltpu.VMEM((SLOTS, SLOTS), BF16)] * 2,
+        out_shape=[square] * 4,
         compiler_params=PARAMS,
         name="weights",
     )(
-        row_slots, ext, ordered_mine, ordered_mate, linv,
+        row_slots, ordered_mine, ordered_mate, linv,
         dinv_diag[None, :], coupled[None, :], coupled_prev[None, :],
     )
-    near, (w_high, w_low, wide) = lax.optimization_barrier((near, weights))
+    near, (w_high, w_low, wd_high, wd_low) = lax.optimization_barrier((near, weights))
     strip_mine = all_y(strip, *near, core)
+    wide = pl.pallas_call(
+        expand_kernel,
+        out_shape=jax.ShapeDtypeStruct((2 * KEXT, SLOTS), BF16),
+        compiler_params=PARAMS,
+        name="expand",
+    )(ext, wd_high, wd_low)
+    strip_mine, wide = lax.optimization_barrier((strip_mine, wide))
     strip_mate = shift(strip_mine, core=1)
     scaled = pl.pallas_call(
         scale_kernel,

time: 156 us -> 152 us (0.974)
  waiting for transfers between devices: 39.3 us -> 29.9 us
  Pallas kernels: 63.9 us -> 69.9 us
    ppermute x16, waiting for transfers between devices: 39.3 us -> 29.9 us  [permute(): return lax.ppermute(value, AXES, pairs)]
    pallas_call x1 -> x2, Pallas kernels: 13.2 us -> 19.3 us  [the longest x1 11.4 us: body(): pl.pallas_call(weight_kernel, out_shape=[square] * 4, compiler_params=PAR...]
  transfers between devices with their start and end apart: 17 -> 17, of which waited for: 11 -> 10; matrix products, arithmetic and copies ran while one was open for 6% -> 7% of each run, Pallas kernels for 18% -> 23%
where the time goes in v1:
time: 152 us
  Pallas kernels  69.9 us (46%)
  waiting for transfers between devices  29.9 us (20%)
  starting transfers between devices  25.4 us (17%)
  between operations  14.4 us (9%)
  local copies, waits for them, and re-layouts  9.73 us (6%)
  other arithmetic  2.83 us (2%)
    ppermute x16, waiting for transfers between devices, permute(): return lax.ppermute(value, AXES, pairs)  29.9 us
    pallas_call x1, Pallas kernels, body(): pl.pallas_call(update_kernel, grid=(rows_blk // tile,), in_specs=[pl.Bloc...  28.3 us
    ppermute x16, starting transfers between devices, permute(): return lax.ppermute(value, AXES, pairs)  25.3 us
    pallas_call x1, Pallas kernels, body(): pl.pallas_call(scale_kernel, out_shape=jax.ShapeDtypeStruct((2 * SLOTS, c...  12.3 us
    pallas_call x1, Pallas kernels, body(): pl.pallas_call(weight_kernel, out_shape=[square] * 4, compiler_params=PAR...  11.4 us
    pallas_call x1, Pallas kernels, body(): pl.pallas_call(expand_kernel, out_shape=jax.ShapeDtypeStruct((2 * KEXT, S...  7.91 us
    pallas_call x1, Pallas kernels, body(): pl.pallas_call(extract_kernel, in_specs=[VM, VM, VM, ANY], out_specs=[VM]...  6.93 us
    unnamed x34, local copies, waits for them, and re-layouts  3.36 us
  transfers between devices with their start and end apart: 17, of which 10 were waited for; matrix products, arithmetic and copies ran while one was open for 7% of the time, Pallas kernels for 23%

profile of v1, /device:TPU:97, one launch (start us, length us, event | category | flops | bytes accessed | tf_op | source)
XLA Modules:
  0.0 152.1 jit_solution(14171306410969906042)
XLA Ops:
  7.2 6.9 %extract.1 = (f32[72,1536]{1,0:T(8,128)}, f32[80,128]{1,0:T(8,128)}, f32[72,768]{1,0:T(8,128)}, f32[72,768]{1,0:T(8,128)}, s32[8,128]{1,0:T(8,128)}, /*index=5*/s32[8,128]{1,0:T(8,128)}) custom-call(s32[8,128]{1,0:T(8,128)} %bitcast.32, s32[1,8]{1,0:T(1,128)} %bitcast.37, f32[8,1536]{1,0:T(8,128)} %delayed_ref.1, f32[1536,768]{1,0:T(8,128)} %front_ref.3), custom_call_target="tpu_custom_call" | custom-call | tf_op jit(solution)/shard_map/extract/pallas_call | solution.py:254
  14.2 2.6 %collective-permute-start.2 = (f32[80,128]{1,0:T(8,128)}, f32[80,128]{1,0:T(8,128)S(1)}, u32[]{:S(2)}, u32[]{:S(2)}) collective-permute-start(f32[80,128]{1,0:T(8,128)} %get-tuple-element.37), channel_id=1, source_target_pairs={{0,3},{1,0},{2,1},{3,2},{4,7},{5,4},{6,5},{7,6},{8,11},{9,8},{10,9... | collective-permute-start | bytes 122888 | tf_op jit(solution)/shard_map/ppermute | solution.py:30
  16.8 0.5 collective-permute-start.1
  17.3 0.6 collective-permute-start
  17.9 0.8 constant_dynamic-update-slice_fusion.3
  18.7 3.1 %collective-permute-done = f32[80,128]{1,0:T(8,128)S(1)} collective-permute-done((f32[80,128]{1,0:T(8,128)}, f32[80,128]{1,0:T(8,128)S(1)}, u32[]{:S(2)}, u32[]{:S(2)}) %collective-permute-start) | collective-permute-done | bytes 40992 | tf_op jit(solution)/shard_map/ppermute | solution.py:30
  21.9 1.9 %collective-permute-start.4 = (f32[320,128]{1,0:T(8,128)S(1)}, f32[320,128]{1,0:T(8,128)S(1)}, u32[]{:S(2)}, u32[]{:S(2)}) collective-permute-start(f32[320,128]{1,0:T(8,128)S(1)} %get-tuple-element.72), channel_id=1, source_target_pairs={{0,8},{1,9},{2,10},{3,11},{4,12},{5,13},{6,14},{7,15},{8,0},{9,1},... | collective-permute-start | bytes 491528 | tf_op jit(solution)/shard_map/ppermute | solution.py:30
  23.8 2.3 %collective-permute-done.3 = f32[320,128]{1,0:T(8,128)S(1)} collective-permute-done((f32[320,128]{1,0:T(8,128)S(1)}, f32[320,128]{1,0:T(8,128)S(1)}, u32[]{:S(2)}, u32[]{:S(2)}) %collective-permute-start.3) | collective-permute-done | bytes 163872 | tf_op jit(solution)/shard_map/ppermute | solution.py:30
  26.1 1.6 %collective-permute-done.4 = f32[320,128]{1,0:T(8,128)S(1)} collective-permute-done((f32[320,128]{1,0:T(8,128)S(1)}, f32[320,128]{1,0:T(8,128)S(1)}, u32[]{:S(2)}, u32[]{:S(2)}) %collective-permute-start.4) | collective-permute-done | bytes 163872 | tf_op jit(solution)/shard_map/ppermute | solution.py:30
  27.7 2.9 %collective-permute-done.5 = f32[320,128]{1,0:T(8,128)S(1)} collective-permute-done((f32[320,128]{1,0:T(8,128)S(1)}, f32[320,128]{1,0:T(8,128)S(1)}, u32[]{:S(2)}, u32[]{:S(2)}) %collective-permute-start.5) | collective-permute-done | bytes 163872 | tf_op jit(solution)/shard_map/ppermute | solution.py:30
  30.8 0.1 pad.18.clone
  30.9 0.1 copy.25
  31.0 0.1 reshape.481
  31.2 0.6 gather_fusion
  31.8 0.7 pad_maximum_fusion.3
  32.6 0.1 copy.23
  32.7 0.6 gather_fusion.2
  33.2 0.1 add_add_fusion
  33.3 0.7 reshape.480.slots_ref
  34.0 3.1 %order.1 = f32[768,128]{1,0:T(8,128)} custom-call(s32[1,1280]{1,0:T(1,128)} %reshape.480.slots_ref, f32[1280,128]{1,0:T(8,128)} %copy-done.6), custom_call_target="tpu_custom_call" | custom-call | tf_op jit(solution)/shard_map/order/pallas_call | solution.py:284
  37.1 2.7 %collective-permute-start.7 = (f32[768,128]{1,0:T(8,128)}, f32[768,128]{1,0:T(8,128)S(1)}, u32[]{:S(2)}, u32[]{:S(2)}) collective-permute-start(f32[768,128]{1,0:T(8,128)} %order.1), channel_id=1, source_target_pairs={{0,96},{1,97},{2,98},{3,99},{4,100},{5,101},{6,102},{7,103},{8,104... | collective-permute-start | bytes 1179656 | tf_op jit(solution)/shard_map/ppermute | solution.py:30
  39.8 0.5 compare_reduce_fusion.1
  40.3 0.6 sub.146.col_ref
  40.9 0.1 pad_add_fusion.pi_slots_ref
  41.0 0.6 gather_fusion.3
  41.5 0.7 reshape.482.slots_ref
  42.2 1.0 compare_reduce_fusion
  43.2 1.1 gather_fusion.1
  44.3 1.0 collective-permute-done.7
  45.4 3.1 %collective-permute-done.6 = f32[768,128]{1,0:T(8,128)S(1)} collective-permute-done((f32[768,128]{1,0:T(8,128)}, f32[768,128]{1,0:T(8,128)S(1)}, u32[]{:S(2)}, u32[]{:S(2)}) %collective-permute-start.6) | collective-permute-done | bytes 393248 | tf_op jit(solution)/shard_map/ppermute | solution.py:30
  48.6 0.4 collective-permute-start.8
  48.9 9.6 %collective-permute-start.9 = (f32[72,768]{1,0:T(8,128)S(1)}, f32[72,768]{1,0:T(8,128)S(1)}, u32[]{:S(2)}, u32[]{:S(2)}) collective-permute-start(f32[72,768]{1,0:T(8,128)S(1)} %copy-done.13), channel_id=1, source_target_pairs={{0,0},{1,1},{2,16},{3,17},{4,32},{5,33},{6,48},{7,49},{8,64},{9,65... | collective-permute-start | bytes 663560 | tf_op jit(solution)/shard_map/ppermute | solution.py:30
  58.6 6.2 %collective-permute-done.9 = f32[72,768]{1,0:T(8,128)S(1)} collective-permute-done((f32[72,768]{1,0:T(8,128)S(1)}, f32[72,768]{1,0:T(8,128)S(1)}, u32[]{:S(2)}, u32[]{:S(2)}) %collective-permute-start.9) | collective-permute-done | bytes 221216 | tf_op jit(solution)/shard_map/ppermute | solution.py:30
  64.8 6.0 %collective-permute-done.10 = f32[72,768]{1,0:T(8,128)S(1)} collective-permute-done((f32[72,768]{1,0:T(8,128)S(1)}, f32[72,768]{1,0:T(8,128)S(1)}, u32[]{:S(2)}, u32[]{:S(2)}) %collective-permute-start.10) | collective-permute-done | bytes 221216 | tf_op jit(solution)/shard_map/ppermute | solution.py:30
  70.8 0.1 pad_maximum_fusion.1.mine_ref
  70.9 3.2 %collective-permute-start.13 = (f32[4,768,128]{2,1,0:T(8,128)S(1)}, f32[4,768,128]{2,1,0:T(8,128)S(1)}, u32[]{:S(2)}, u32[]{:S(2)}) collective-permute-start(f32[4,768,128]{2,1,0:T(8,128)S(1)} %pad_maximum_fusion.1.mine_ref), channel_id=1, source_target_pairs={{0,16},{1,17},{2,18},{3,19},{4,20},{5,21},{6,22},{7,23},{8,24},{9,... | collective-permute-start | bytes 4718600 | tf_op jit(solution)/shard_map/ppermute | solution.py:30
  74.1 1.5 collective-permute-start.11
  75.6 1.6 %collective-permute-done.13.mate_ref = f32[4,768,128]{2,1,0:T(8,128)S(1)} collective-permute-done((f32[4,768,128]{2,1,0:T(8,128)S(1)}, f32[4,768,128]{2,1,0:T(8,128)S(1)}, u32[]{:S(2)}, u32[]{:S(2)}) %collective-permute-start.13) | collective-permute-done | bytes 1572896 | tf_op jit(solution)/shard_map/ppermute | solution.py:30
  77.2 1.1 copy-done.4
  78.3 11.4 %weights.1 = (bf16[1024,1024]{1,0:T(8,128)(2,1)}, bf16[1024,1024]{1,0:T(8,128)(2,1)}, bf16[1024,1024]{1,0:T(8,128)(2,1)}, bf16[1024,1024]{1,0:T(8,128)(2,1)}) custom-call(s32[8,128]{1,0:T(8,128)} %gather_fusion.1, f32[4,768,128]{2,1,0:T(8,128)} %copy-done.1, f32[4,768,128]{2,1,0:T(8,128)} %copy-done.4, f32[4,256,256]{2,1,0:T(8,128)} %linv_ref.1, ...), custom_call_target="tpu_custom_call" | custom-call | tf_op jit(solution)/shard_map/weights/pallas_call | solution.py:327
  89.8 7.9 %expand.1.wide_ref = bf16[2304,1024]{1,0:T(8,128)(2,1)} custom-call(s32[16,72]{1,0:T(8,128)} %copy-done.5, bf16[1024,1024]{1,0:T(8,128)(2,1)} %get-tuple-element.63.dh_ref, bf16[1024,1024]{1,0:T(8,128)(2,1)} %get-tuple-element.64.dl_ref), custom_call_target="tpu_custom_call" | custom-call | tf_op jit(solution)/shard_map/expand/pallas_call | solution.py:338
  97.7 0.1 pad_maximum_fusion.mine_ref
  97.9 2.2 %collective-permute-start.15 = (f32[4,144,768]{2,1,0:T(8,128)S(1)}, f32[4,144,768]{2,1,0:T(8,128)S(1)}, u32[]{:S(2)}, u32[]{:S(2)}) collective-permute-start(f32[4,144,768]{2,1,0:T(8,128)S(1)} %pad_maximum_fusion.mine_ref), channel_id=1, source_target_pairs={{0,16},{1,17},{2,18},{3,19},{4,20},{5,21},{6,22},{7,23},{8,24},{9,... | collective-permute-start | bytes 5308424 | tf_op jit(solution)/shard_map/ppermute | solution.py:30
  100.1 1.2 copy.26.row_ref
  101.3 2.1 %collective-permute-done.15.mate_ref = f32[4,144,768]{2,1,0:T(8,128)S(1)} collective-permute-done((f32[4,144,768]{2,1,0:T(8,128)S(1)}, f32[4,144,768]{2,1,0:T(8,128)S(1)}, u32[]{:S(2)}, u32[]{:S(2)}) %collective-permute-start.15) | collective-permute-done | bytes 1769504 | tf_op jit(solution)/shard_map/ppermute | solution.py:30
  103.4 1.2 copy-done.2
  104.6 12.3 %scale.1.scaled_ref = bf16[2048,768]{1,0:T(8,128)(2,1)} custom-call(s32[1,1152]{1,0:T(1,128)} %reshape.482.slots_ref, f32[4,144,768]{2,1,0:T(8,128)} %copy-done, f32[4,144,768]{2,1,0:T(8,128)} %copy-done.2, bf16[1024,1024]{1,0:T(8,128)(2,1)} %get-tuple-element.68.wh_ref, bf16[1024,1024]{1,0:T(8,128)(2,1)} %get-tuple-element.69.wl_ref), custom_call_target="tpu_custom_call" | custom-call | tf_op jit(solution)/shard_map/scale/pallas_call | solution.py:346
  117.0 28.3 %update.1 = (f32[1536,768]{1,0:T(8,128)}, f32[1536,1024]{1,0:T(8,128)}) custom-call(f32[1152,1536]{1,0:T(8,128)} %all-gather.2.cloned.1.call-done.piece_ref, bf16[2304,1024]{1,0:T(8,128)(2,1)} %expand.1.wide_ref, bf16[2048,768]{1,0:T(8,128)(2,1)} %scale.1.scaled_ref, f32[1536,768]{1,0:T(8,128)} %front_ref.3, f32[1536,1]{1,0:T(8,128)} %copy.26.row_ref, ...), custom_call_target="tpu_custom_call" | custom-call | tf_op jit(solution)/shard_map/update/pallas_call | solution.py:355
  (69 shorter events, 0.8 us)
Async XLA Ops:
  7.2 109.8 %all-gather.2.cloned.1.call-start = ((), (), s32[]{:S(2)}) async-start(), calls=%async_computation | async-start | bytes 7520256 | tf_op jit(solution)/shard_map/all_gather | solution.py:274
  14.1 16.9 %copy-start.7 = (s32[8,128]{1,0:T(8,128)S(1)}, s32[8,128]{1,0:T(8,128)}, u32[]{:S(2)}) copy-start(s32[8,128]{1,0:T(8,128)} %get-tuple-element.45) | copy-start | bytes 12292
  14.2 17.6 %copy-start.10 = (f32[1024]{0:T(1024)S(1)}, f32[1024]{0:T(1024)}, u32[]{:S(2)}) copy-start(f32[1024]{0:T(1024)} %param.15) | copy-start | bytes 12292
  14.2 17.6 %copy-start.11 = (s32[1024]{0:T(1024)S(1)}, s32[1024]{0:T(1024)}, u32[]{:S(2)}) copy-start(s32[1024]{0:T(1024)} %param.12) | copy-start | bytes 12292
  14.2 25.6 %copy-start.8 = (s32[1024]{0:T(1024)S(1)}, s32[1024]{0:T(1024)}, u32[]{:S(2)}) copy-start(s32[1024]{0:T(1024)} %param.11) | copy-start | bytes 12292
  14.2 7.6 %collective-permute-start.2 = (f32[80,128]{1,0:T(8,128)}, f32[80,128]{1,0:T(8,128)S(1)}, u32[]{:S(2)}, u32[]{:S(2)}) collective-permute-start(f32[80,128]{1,0:T(8,128)} %get-tuple-element.37), channel_id=1, source_target_pairs={{0,3},{1,0},{2,1},{3,2},{4,7},{5,4},{6,5},{7,6},{8,11},{9,8},{10,9... | collective-permute-start | bytes 122888 | tf_op jit(solution)/shard_map/ppermute | solution.py:30
  16.8 5.0 %collective-permute-start.1 = (f32[80,128]{1,0:T(8,128)}, f32[80,128]{1,0:T(8,128)S(1)}, u32[]{:S(2)}, u32[]{:S(2)}) collective-permute-start(f32[80,128]{1,0:T(8,128)} %get-tuple-element.37), channel_id=1, source_target_pairs={{0,2},{1,3},{2,0},{3,1},{4,6},{5,7},{6,4},{7,5},{8,10},{9,11},{10,... | collective-permute-start | bytes 122888 | tf_op jit(solution)/shard_map/ppermute | solution.py:30
  17.3 4.5 %collective-permute-start = (f32[80,128]{1,0:T(8,128)}, f32[80,128]{1,0:T(8,128)S(1)}, u32[]{:S(2)}, u32[]{:S(2)}) collective-permute-start(f32[80,128]{1,0:T(8,128)} %get-tuple-element.37), channel_id=1, source_target_pairs={{0,1},{1,2},{2,3},{3,0},{4,5},{5,6},{6,7},{7,4},{8,9},{9,10},{10,1... | collective-permute-start | bytes 122888 | tf_op jit(solution)/shard_map/ppermute | solution.py:30
  21.8 4.2 %collective-permute-start.3 = (f32[320,128]{1,0:T(8,128)S(1)}, f32[320,128]{1,0:T(8,128)S(1)}, u32[]{:S(2)}, u32[]{:S(2)}) collective-permute-start(f32[320,128]{1,0:T(8,128)S(1)} %get-tuple-element.72), channel_id=1, source_target_pairs={{0,4},{1,5},{2,6},{3,7},{4,8},{5,9},{6,10},{7,11},{8,12},{9,13},{1... | collective-permute-start | bytes 491528 | tf_op jit(solution)/shard_map/ppermute | solution.py:30
  21.9 5.8 %collective-permute-start.4 = (f32[320,128]{1,0:T(8,128)S(1)}, f32[320,128]{1,0:T(8,128)S(1)}, u32[]{:S(2)}, u32[]{:S(2)}) collective-permute-start(f32[320,128]{1,0:T(8,128)S(1)} %get-tuple-element.72), channel_id=1, source_target_pairs={{0,8},{1,9},{2,10},{3,11},{4,12},{5,13},{6,14},{7,15},{8,0},{9,1},... | collective-permute-start | bytes 491528 | tf_op jit(solution)/shard_map/ppermute | solution.py:30
  23.8 6.9 %collective-permute-start.5 = (f32[320,128]{1,0:T(8,128)S(1)}, f32[320,128]{1,0:T(8,128)S(1)}, u32[]{:S(2)}, u32[]{:S(2)}) collective-permute-start(f32[320,128]{1,0:T(8,128)S(1)} %get-tuple-element.72), channel_id=1, source_target_pairs={{0,12},{1,13},{2,14},{3,15},{4,0},{5,1},{6,2},{7,3},{8,4},{9,5},{1... | collective-permute-start | bytes 491528 | tf_op jit(solution)/shard_map/ppermute | solution.py:30
  27.7 21.2 %copy-start.13 = (f32[72,768]{1,0:T(8,128)S(1)}, f32[72,768]{1,0:T(8,128)}, u32[]{:S(2)}) copy-start(f32[72,768]{1,0:T(8,128)} %get-tuple-element.49) | copy-start | bytes 663556
  27.7 30.8 %copy-start.12 = (f32[72,768]{1,0:T(8,128)S(1)}, f32[72,768]{1,0:T(8,128)}, u32[]{:S(2)}) copy-start(f32[72,768]{1,0:T(8,128)} %get-tuple-element.50) | copy-start | bytes 663556
  30.7 3.3 %copy-start.6 = (f32[1280,128]{1,0:T(8,128)}, f32[1280,128]{1,0:T(8,128)S(1)}, u32[]{:S(2)}) copy-start(f32[1280,128]{1,0:T(8,128)S(1)} %constant_dynamic-update-slice_fusion.4.crossing_ref) | copy-start | bytes 1966084
  31.8 39.1 %copy-start.9 = (f32[1024]{0:T(1024)}, f32[1024]{0:T(1024)S(1)}, u32[]{:S(2)}) copy-start(f32[1024]{0:T(1024)S(1)} %convert_multiply_fusion) | copy-start | bytes 12292
  37.0 33.7 %copy-start.3 = (f32[768,128]{1,0:T(8,128)S(1)}, f32[768,128]{1,0:T(8,128)}, u32[]{:S(2)}) copy-start(f32[768,128]{1,0:T(8,128)} %order.1) | copy-start | bytes 1179652
  37.1 8.3 %collective-permute-start.7 = (f32[768,128]{1,0:T(8,128)}, f32[768,128]{1,0:T(8,128)S(1)}, u32[]{:S(2)}, u32[]{:S(2)}) collective-permute-start(f32[768,128]{1,0:T(8,128)} %order.1), channel_id=1, source_target_pairs={{0,96},{1,97},{2,98},{3,99},{4,100},{5,101},{6,102},{7,103},{8,104... | collective-permute-start | bytes 1179656 | tf_op jit(solution)/shard_map/ppermute | solution.py:30
  39.8 8.7 %collective-permute-start.6 = (f32[768,128]{1,0:T(8,128)}, f32[768,128]{1,0:T(8,128)S(1)}, u32[]{:S(2)}, u32[]{:S(2)}) collective-permute-start(f32[768,128]{1,0:T(8,128)} %order.1), channel_id=1, source_target_pairs={{0,32},{1,33},{2,34},{3,35},{4,36},{5,37},{6,38},{7,39},{8,40},{9,... | collective-permute-start | bytes 1179656 | tf_op jit(solution)/shard_map/ppermute | solution.py:30
  41.0 30.0 %copy-start.5 = (s32[16,72]{1,0:T(8,128)}, s32[16,72]{1,0:T(8,128)S(1)}, u32[]{:S(2)}) copy-start(s32[16,72]{1,0:T(8,128)S(1)} %pad_add_fusion.pi_slots_ref) | copy-start | bytes 13828
  48.6 22.2 %collective-permute-start.8 = (f32[768,128]{1,0:T(8,128)S(1)}, f32[768,128]{1,0:T(8,128)S(1)}, u32[]{:S(2)}, u32[]{:S(2)}) collective-permute-start(f32[768,128]{1,0:T(8,128)S(1)} %broadcast_select_fusion.1), channel_id=1, source_target_pairs={{0,32},{1,33},{2,34},{3,35},{4,36},{5,37},{6,38},{7,39},{8,40},{9,... | collective-permute-start | bytes 1179656 | tf_op jit(solution)/shard_map/ppermute | solution.py:30
  48.9 15.9 %collective-permute-start.9 = (f32[72,768]{1,0:T(8,128)S(1)}, f32[72,768]{1,0:T(8,128)S(1)}, u32[]{:S(2)}, u32[]{:S(2)}) collective-permute-start(f32[72,768]{1,0:T(8,128)S(1)} %copy-done.13), channel_id=1, source_target_pairs={{0,0},{1,1},{2,16},{3,17},{4,32},{5,33},{6,48},{7,49},{8,64},{9,65... | collective-permute-start | bytes 663560 | tf_op jit(solution)/shard_map/ppermute | solution.py:30
  58.5 12.2 %collective-permute-start.10 = (f32[72,768]{1,0:T(8,128)S(1)}, f32[72,768]{1,0:T(8,128)S(1)}, u32[]{:S(2)}, u32[]{:S(2)}) collective-permute-start(f32[72,768]{1,0:T(8,128)S(1)} %copy-done.12), channel_id=1, source_target_pairs={{0,1},{1,0},{2,17},{3,16},{4,33},{5,32},{6,49},{7,48},{8,65},{9,64... | collective-permute-start | bytes 663560 | tf_op jit(solution)/shard_map/ppermute | solution.py:30
  70.9 6.2 %copy-start.1 = (f32[4,768,128]{2,1,0:T(8,128)}, f32[4,768,128]{2,1,0:T(8,128)S(1)}, u32[]{:S(2)}) copy-start(f32[4,768,128]{2,1,0:T(8,128)S(1)} %pad_maximum_fusion.1.mine_ref) | copy-start | bytes 4718596
  70.9 6.2 %collective-permute-start.13 = (f32[4,768,128]{2,1,0:T(8,128)S(1)}, f32[4,768,128]{2,1,0:T(8,128)S(1)}, u32[]{:S(2)}, u32[]{:S(2)}) collective-permute-start(f32[4,768,128]{2,1,0:T(8,128)S(1)} %pad_maximum_fusion.1.mine_ref), channel_id=1, source_target_pairs={{0,16},{1,17},{2,18},{3,19},{4,20},{5,21},{6,22},{7,23},{8,24},{9,... | collective-permute-start | bytes 4718600 | tf_op jit(solution)/shard_map/ppermute | solution.py:30
  74.1 15.5 %collective-permute-start.12 = (f32[144,768]{1,0:T(8,128)S(1)}, f32[144,768]{1,0:T(8,128)S(1)}, u32[]{:S(2)}, u32[]{:S(2)}) collective-permute-start(f32[144,768]{1,0:T(8,128)S(1)} %pad_maximum_fusion.2), channel_id=1, source_target_pairs={{0,96},{1,97},{2,98},{3,99},{4,100},{5,101},{6,102},{7,103},{8,104... | collective-permute-start | bytes 1327112 | tf_op jit(solution)/shard_map/ppermute | solution.py:30
  74.1 15.5 %collective-permute-start.11 = (f32[144,768]{1,0:T(8,128)S(1)}, f32[144,768]{1,0:T(8,128)S(1)}, u32[]{:S(2)}, u32[]{:S(2)}) collective-permute-start(f32[144,768]{1,0:T(8,128)S(1)} %pad_maximum_fusion.2), channel_id=1, source_target_pairs={{0,32},{1,33},{2,34},{3,35},{4,36},{5,37},{6,38},{7,39},{8,40},{9,... | collective-permute-start | bytes 1327112 | tf_op jit(solution)/shard_map/ppermute | solution.py:30
  77.2 1.1 copy-start.4
  89.7 8.0 %collective-permute-start.14 = (f32[144,768]{1,0:T(8,128)S(1)}, f32[144,768]{1,0:T(8,128)S(1)}, u32[]{:S(2)}, u32[]{:S(2)}) collective-permute-start(f32[144,768]{1,0:T(8,128)S(1)} %broadcast_select_fusion), channel_id=1, source_target_pairs={{0,32},{1,33},{2,34},{3,35},{4,36},{5,37},{6,38},{7,39},{8,40},{9,... | collective-permute-start | bytes 1327112 | tf_op jit(solution)/shard_map/ppermute | solution.py:30
  97.9 5.5 %copy-start = (f32[4,144,768]{2,1,0:T(8,128)}, f32[4,144,768]{2,1,0:T(8,128)S(1)}, u32[]{:S(2)}) copy-start(f32[4,144,768]{2,1,0:T(8,128)S(1)} %pad_maximum_fusion.mine_ref) | copy-start | bytes 5308420
  97.9 5.5 %collective-permute-start.15 = (f32[4,144,768]{2,1,0:T(8,128)S(1)}, f32[4,144,768]{2,1,0:T(8,128)S(1)}, u32[]{:S(2)}, u32[]{:S(2)}) collective-permute-start(f32[4,144,768]{2,1,0:T(8,128)S(1)} %pad_maximum_fusion.mine_ref), channel_id=1, source_target_pairs={{0,16},{1,17},{2,18},{3,19},{4,20},{5,21},{6,22},{7,23},{8,24},{9,... | collective-permute-start | bytes 5308424 | tf_op jit(solution)/shard_map/ppermute | solution.py:30
  103.4 1.2 copy-start.2
Sparse Core Ops, SparseCore 0:
  30.8 73.9 all-gather.1

commit v2 on v1

--- a/solution.py
+++ b/solution.py
@@ -49,6 +49,11 @@
 
 def near_y(block):
     return shift(block, y=1), shift(block, y=-1)
+
+
+def far_y(behind, ahead, core):
+    relay = jnp.where(core == 0, behind, ahead)
+    return permute(relay, lambda r, c: ((r // 2 + (1 if r % 2 == 0 else -1)) % 4 * 2 + r % 2, c))
 
 
 def all_y(block, behind, ahead, core):
@@ -207,8 +212,13 @@
             wide_ref[low_rows, cols] = mm(pick[:, :depth], dl_ref[:depth, cols]).astype(BF16)
 
 
-def scale_kernel(slots_ref, mine_ref, mate_ref, wh_ref, wl_ref, out_ref, ph_ref, pl_ref):
-    got = jnp.concatenate([mine_ref[i] for i in range(4)] + [mate_ref[i] for i in range(4)], axis=0)
+def scale_kernel(
+    slots_ref, mine_ref, far_ref, mate_ref, far_mate_ref, wh_ref, wl_ref, out_ref, ph_ref, pl_ref
+):
+    got = jnp.concatenate(
+        [mine_ref[i] for i in range(3)] + [far_ref[...]] + [mate_ref[i] for i in range(3)] + [far_mate_ref[...]],
+        axis=0,
+    )
     got_h, got_l = split(got)
     for p in range(PANELS):
         rows = slice(p * PANEL, (p + 1) * PANEL)
@@ -307,7 +317,9 @@
     row_slots = slot_at[row_source]
     coupled = pair_flags.astype(F32) * dinv_off
     coupled_prev = jnp.concatenate([jnp.zeros_like(coupled[:1]), coupled[:-1]])
-    first = (row_source // 2 - z) % 4 * 4 + row_source % 2 * 2
+    away = jnp.where(rel_row % 4 < 2, rel_row % 4, 5 - rel_row % 4)
+    strip_source = (y - away) % 4 * 2 + (core + rel_row // 4) % 2
+    first = (strip_source // 2 - z) % 4 * 4 + strip_source % 2 * 2
     pair = jnp.stack([first + parity, first + 1 - parity], axis=1).reshape(COLS)
     pair_slots = ext[pair].reshape(1, KEXT)
     row_ids = r * rows_blk + jnp.arange(rows_blk, dtype=jnp.int32)
@@ -334,22 +346,24 @@
         dinv_diag[None, :], coupled[None, :], coupled_prev[None, :],
     )
     near, (w_high, w_low, wd_high, wd_low) = lax.optimization_barrier((near, weights))
-    strip_mine = all_y(strip, *near, core)
+    strip_mine = jnp.stack([strip, *near], axis=0)
+    strip_mate = shift(strip_mine, core=1)
+    strip_far = far_y(*near, core)
     wide = pl.pallas_call(
         expand_kernel,
         out_shape=jax.ShapeDtypeStruct((2 * KEXT, SLOTS), BF16),
         compiler_params=PARAMS,
         name="expand",
     )(ext, wd_high, wd_low)
-    strip_mine, wide = lax.optimization_barrier((strip_mine, wide))
-    strip_mate = shift(strip_mine, core=1)
+    strip_far, wide = lax.optimization_barrier((strip_far, wide))
+    strip_far_mate = shift(strip_far, core=1)
     scaled = pl.pallas_call(
         scale_kernel,
         out_shape=jax.ShapeDtypeStruct((2 * SLOTS, cols_blk), BF16),
         scratch_shapes=[pltpu.VMEM((SLOTS, cols_blk), BF16)] * 2,
         compiler_params=PARAMS,
         name="scale",
-    )(pair_slots, strip_mine, strip_mate, w_high, w_low)
+    )(pair_slots, strip_mine, strip_far, strip_mate, strip_far_mate, w_high, w_low)
 
     tile = 2 * TILE
     trailing, factor = pl.pallas_call(

time: 152 us -> 151 us (level)
  waiting for transfers between devices: 29.9 us -> 27.9 us
    ppermute x16 -> x17, waiting for transfers between devices: 29.9 us -> 27.9 us  [permute(): return lax.ppermute(value, AXES, pairs)]
    unnamed x34 -> x38, local copies, waits for them, and re-layouts: 3.36 us -> 4.06 us
    ppermute x16 -> x17, starting transfers between devices: 25.3 us -> 25.3 us  [permute(): return lax.ppermute(value, AXES, pairs)]
  transfers between devices with their start and end apart: 17 -> 18, of which waited for: 10 -> 10; matrix products, arithmetic and copies ran while one was open for 7% -> 7% of each run, Pallas kernels for 23% -> 23%
where the time goes in v2:
time: 151 us
  Pallas kernels  69.9 us (46%)
  waiting for transfers between devices  27.9 us (18%)
  starting transfers between devices  25.3 us (17%)
  between operations  14.4 us (10%)
  local copies, waits for them, and re-layouts  10.5 us (7%)
  other arithmetic  2.79 us (2%)
    pallas_call x1, Pallas kernels, body(): pl.pallas_call(update_kernel, grid=(rows_blk // tile,), in_specs=[pl.Bloc...  28.3 us
    ppermute x17, waiting for transfers between devices, permute(): return lax.ppermute(value, AXES, pairs)  27.9 us
    ppermute x17, starting transfers between devices, permute(): return lax.ppermute(value, AXES, pairs)  25.3 us
    pallas_call x1, Pallas kernels, body(): pl.pallas_call(scale_kernel, out_shape=jax.ShapeDtypeStruct((2 * SLOTS, c...  12.3 us
    pallas_call x1, Pallas kernels, body(): pl.pallas_call(weight_kernel, out_shape=[square] * 4, compiler_params=PAR...  11.3 us
    pallas_call x1, Pallas kernels, body(): pl.pallas_call(expand_kernel, out_shape=jax.ShapeDtypeStruct((2 * KEXT, S...  7.94 us
    pallas_call x1, Pallas kernels, body(): pl.pallas_call(extract_kernel, in_specs=[VM, VM, VM, ANY], out_specs=[VM]...  6.96 us
    unnamed x38, local copies, waits for them, and re-layouts  4.06 us
  transfers between devices with their start and end apart: 18, of which 10 were waited for; matrix products, arithmetic and copies ran while one was open for 7% of the time, Pallas kernels for 23%

profile of v2, /device:TPU:97, one launch (start us, length us, event | category | flops | bytes accessed | tf_op | source)
XLA Modules:
  0.0 150.9 jit_solution(12353045574572997587)
XLA Ops:
  7.2 7.0 %extract.1 = (f32[72,1536]{1,0:T(8,128)}, f32[80,128]{1,0:T(8,128)}, f32[72,768]{1,0:T(8,128)}, f32[72,768]{1,0:T(8,128)}, s32[8,128]{1,0:T(8,128)}, /*index=5*/s32[8,128]{1,0:T(8,128)}) custom-call(s32[8,128]{1,0:T(8,128)} %bitcast.30, s32[1,8]{1,0:T(1,128)} %bitcast.35, f32[8,1536]{1,0:T(8,128)} %delayed_ref.1, f32[1536,768]{1,0:T(8,128)} %front_ref.3), custom_call_target="tpu_custom_call" | custom-call | tf_op jit(solution)/shard_map/extract/pallas_call | solution.py:264
  14.2 2.6 %collective-permute-start.2 = (f32[80,128]{1,0:T(8,128)}, f32[80,128]{1,0:T(8,128)S(1)}, u32[]{:S(2)}, u32[]{:S(2)}) collective-permute-start(f32[80,128]{1,0:T(8,128)} %get-tuple-element.37), channel_id=1, source_target_pairs={{0,3},{1,0},{2,1},{3,2},{4,7},{5,4},{6,5},{7,6},{8,11},{9,8},{10,9... | collective-permute-start | bytes 122888 | tf_op jit(solution)/shard_map/ppermute | solution.py:30
  16.8 0.5 collective-permute-start.1
  17.3 0.6 collective-permute-start
  17.9 0.8 constant_dynamic-update-slice_fusion.3
  18.7 3.1 %collective-permute-done = f32[80,128]{1,0:T(8,128)S(1)} collective-permute-done((f32[80,128]{1,0:T(8,128)}, f32[80,128]{1,0:T(8,128)S(1)}, u32[]{:S(2)}, u32[]{:S(2)}) %collective-permute-start) | collective-permute-done | bytes 40992 | tf_op jit(solution)/shard_map/ppermute | solution.py:30
  21.9 1.9 %collective-permute-start.4 = (f32[320,128]{1,0:T(8,128)S(1)}, f32[320,128]{1,0:T(8,128)S(1)}, u32[]{:S(2)}, u32[]{:S(2)}) collective-permute-start(f32[320,128]{1,0:T(8,128)S(1)} %get-tuple-element.72), channel_id=1, source_target_pairs={{0,8},{1,9},{2,10},{3,11},{4,12},{5,13},{6,14},{7,15},{8,0},{9,1},... | collective-permute-start | bytes 491528 | tf_op jit(solution)/shard_map/ppermute | solution.py:30
  23.8 2.3 %collective-permute-done.3 = f32[320,128]{1,0:T(8,128)S(1)} collective-permute-done((f32[320,128]{1,0:T(8,128)S(1)}, f32[320,128]{1,0:T(8,128)S(1)}, u32[]{:S(2)}, u32[]{:S(2)}) %collective-permute-start.3) | collective-permute-done | bytes 163872 | tf_op jit(solution)/shard_map/ppermute | solution.py:30
  26.1 1.6 %collective-permute-done.4 = f32[320,128]{1,0:T(8,128)S(1)} collective-permute-done((f32[320,128]{1,0:T(8,128)S(1)}, f32[320,128]{1,0:T(8,128)S(1)}, u32[]{:S(2)}, u32[]{:S(2)}) %collective-permute-start.4) | collective-permute-done | bytes 163872 | tf_op jit(solution)/shard_map/ppermute | solution.py:30
  27.7 2.9 %collective-permute-done.5 = f32[320,128]{1,0:T(8,128)S(1)} collective-permute-done((f32[320,128]{1,0:T(8,128)S(1)}, f32[320,128]{1,0:T(8,128)S(1)}, u32[]{:S(2)}, u32[]{:S(2)}) %collective-permute-start.5) | collective-permute-done | bytes 163872 | tf_op jit(solution)/shard_map/ppermute | solution.py:30
  30.8 0.1 pad.17.clone
  30.9 0.1 copy.25
  31.0 0.1 reshape.535
  31.2 0.6 gather_fusion
  31.9 0.7 pad_maximum_fusion.3
  32.7 0.6 gather_fusion.2
  33.3 0.1 add_add_fusion
  33.4 0.7 reshape.534.slots_ref
  34.1 3.1 %order.1 = f32[768,128]{1,0:T(8,128)} custom-call(s32[1,1280]{1,0:T(1,128)} %reshape.534.slots_ref, f32[1280,128]{1,0:T(8,128)} %copy-done.6), custom_call_target="tpu_custom_call" | custom-call | tf_op jit(solution)/shard_map/order/pallas_call | solution.py:294
  37.1 2.7 %collective-permute-start.7 = (f32[768,128]{1,0:T(8,128)}, f32[768,128]{1,0:T(8,128)S(1)}, u32[]{:S(2)}, u32[]{:S(2)}) collective-permute-start(f32[768,128]{1,0:T(8,128)} %order.1), channel_id=1, source_target_pairs={{0,96},{1,97},{2,98},{3,99},{4,100},{5,101},{6,102},{7,103},{8,104... | collective-permute-start | bytes 1179656 | tf_op jit(solution)/shard_map/ppermute | solution.py:30
  39.8 0.5 compare_reduce_fusion.1
  40.4 0.6 sub.170.col_ref
  41.0 0.6 gather_fusion.3
  41.6 0.7 reshape.536.slots_ref
  42.3 1.0 compare_reduce_fusion
  43.3 1.1 gather_fusion.1
  44.4 1.0 collective-permute-done.7
  45.4 3.1 %collective-permute-done.6 = f32[768,128]{1,0:T(8,128)S(1)} collective-permute-done((f32[768,128]{1,0:T(8,128)}, f32[768,128]{1,0:T(8,128)S(1)}, u32[]{:S(2)}, u32[]{:S(2)}) %collective-permute-start.6) | collective-permute-done | bytes 393248 | tf_op jit(solution)/shard_map/ppermute | solution.py:30
  48.6 0.4 collective-permute-start.8
  49.0 9.6 %collective-permute-start.9 = (f32[72,768]{1,0:T(8,128)S(1)}, f32[72,768]{1,0:T(8,128)S(1)}, u32[]{:S(2)}, u32[]{:S(2)}) collective-permute-start(f32[72,768]{1,0:T(8,128)S(1)} %copy-done.15), channel_id=1, source_target_pairs={{0,0},{1,1},{2,16},{3,17},{4,32},{5,33},{6,48},{7,49},{8,64},{9,65... | collective-permute-start | bytes 663560 | tf_op jit(solution)/shard_map/ppermute | solution.py:30
  58.7 6.2 %collective-permute-done.9 = f32[72,768]{1,0:T(8,128)S(1)} collective-permute-done((f32[72,768]{1,0:T(8,128)S(1)}, f32[72,768]{1,0:T(8,128)S(1)}, u32[]{:S(2)}, u32[]{:S(2)}) %collective-permute-start.9) | collective-permute-done | bytes 221216 | tf_op jit(solution)/shard_map/ppermute | solution.py:30
  64.8 6.0 %collective-permute-done.10 = f32[72,768]{1,0:T(8,128)S(1)} collective-permute-done((f32[72,768]{1,0:T(8,128)S(1)}, f32[72,768]{1,0:T(8,128)S(1)}, u32[]{:S(2)}, u32[]{:S(2)}) %collective-permute-start.10) | collective-permute-done | bytes 221216 | tf_op jit(solution)/shard_map/ppermute | solution.py:30
  70.9 0.1 pad_maximum_fusion.mine_ref
  71.0 3.2 %collective-permute-start.13 = (f32[4,768,128]{2,1,0:T(8,128)S(1)}, f32[4,768,128]{2,1,0:T(8,128)S(1)}, u32[]{:S(2)}, u32[]{:S(2)}) collective-permute-start(f32[4,768,128]{2,1,0:T(8,128)S(1)} %pad_maximum_fusion.mine_ref), channel_id=1, source_target_pairs={{0,16},{1,17},{2,18},{3,19},{4,20},{5,21},{6,22},{7,23},{8,24},{9,... | collective-permute-start | bytes 4718600 | tf_op jit(solution)/shard_map/ppermute | solution.py:30
  74.2 1.5 collective-permute-start.11
  75.7 1.6 %collective-permute-done.13.mate_ref = f32[4,768,128]{2,1,0:T(8,128)S(1)} collective-permute-done((f32[4,768,128]{2,1,0:T(8,128)S(1)}, f32[4,768,128]{2,1,0:T(8,128)S(1)}, u32[]{:S(2)}, u32[]{:S(2)}) %collective-permute-start.13) | collective-permute-done | bytes 1572896 | tf_op jit(solution)/shard_map/ppermute | solution.py:30
  77.2 1.2 copy-done.3
  78.5 11.3 %weights.1 = (bf16[1024,1024]{1,0:T(8,128)(2,1)}, bf16[1024,1024]{1,0:T(8,128)(2,1)}, bf16[1024,1024]{1,0:T(8,128)(2,1)}, bf16[1024,1024]{1,0:T(8,128)(2,1)}) custom-call(s32[8,128]{1,0:T(8,128)} %gather_fusion.1, f32[4,768,128]{2,1,0:T(8,128)} %copy-done, f32[4,768,128]{2,1,0:T(8,128)} %copy-done.3, f32[4,256,256]{2,1,0:T(8,128)} %linv_ref.1, ...), custom_call_target="tpu_custom_call" | custom-call | tf_op jit(solution)/shard_map/weights/pallas_call | solution.py:339
  89.8 0.1 pad_maximum_fusion.1.mine_ref
  90.0 0.4 collective-permute-start.15
  90.5 7.9 %expand.1.wide_ref = bf16[2304,1024]{1,0:T(8,128)(2,1)} custom-call(s32[16,72]{1,0:T(8,128)} %copy-done.5, bf16[1024,1024]{1,0:T(8,128)(2,1)} %get-tuple-element.63.dh_ref, bf16[1024,1024]{1,0:T(8,128)(2,1)} %get-tuple-element.64.dl_ref), custom_call_target="tpu_custom_call" | custom-call | tf_op jit(solution)/shard_map/expand/pallas_call | solution.py:352
  98.4 1.8 %collective-permute-start.16 = (f32[144,768]{1,0:T(8,128)S(1)}, f32[144,768]{1,0:T(8,128)S(1)}, u32[]{:S(2)}, u32[]{:S(2)}) collective-permute-start(f32[144,768]{1,0:T(8,128)S(1)} %collective-permute-done.14.far_ref), channel_id=1, source_target_pairs={{0,16},{1,17},{2,18},{3,19},{4,20},{5,21},{6,22},{7,23},{8,24},{9,... | collective-permute-start | bytes 1327112 | tf_op jit(solution)/shard_map/ppermute | solution.py:30
  100.2 1.3 copy.26.row_ref
  101.4 0.2 collective-permute-done.16.far_mate_ref
  101.6 0.7 copy-done.8
  102.4 1.1 copy-done.4
  103.4 12.3 %scale.1.scaled_ref = bf16[2048,768]{1,0:T(8,128)(2,1)} custom-call(s32[1,1152]{1,0:T(1,128)} %reshape.536.slots_ref, f32[3,144,768]{2,1,0:T(8,128)} %copy-done.1, f32[144,768]{1,0:T(8,128)} %copy-done.7, f32[3,144,768]{2,1,0:T(8,128)} %copy-done.4, f32[144,768]{1,0:T(8,128)} %copy-done.8, bf16[1024,1024]{1,0:T(8,128)(2,1)} %get-tuple-element.68.wh_ref, ...), custom_call_target="tpu_custom_call" | custom-call | tf_op jit(solution)/shard_map/scale/pallas_call | solution.py:360
  115.7 28.3 %update.1 = (f32[1536,768]{1,0:T(8,128)}, f32[1536,1024]{1,0:T(8,128)}) custom-call(f32[1152,1536]{1,0:T(8,128)} %all-gather.2.cloned.1.call-done.piece_ref, bf16[2304,1024]{1,0:T(8,128)(2,1)} %expand.1.wide_ref, bf16[2048,768]{1,0:T(8,128)(2,1)} %scale.1.scaled_ref, f32[1536,768]{1,0:T(8,128)} %front_ref.3, f32[1536,1]{1,0:T(8,128)} %copy.26.row_ref, ...), custom_call_target="tpu_custom_call" | custom-call | tf_op jit(solution)/shard_map/update/pallas_call | solution.py:369
  (75 shorter events, 1.0 us)
Async XLA Ops:
  7.2 108.6 %all-gather.2.cloned.1.call-start = ((), (), s32[]{:S(2)}) async-start(), calls=%async_computation | async-start | bytes 7520256 | tf_op jit(solution)/shard_map/all_gather | solution.py:284
  14.2 16.9 %copy-start.9 = (s32[8,128]{1,0:T(8,128)S(1)}, s32[8,128]{1,0:T(8,128)}, u32[]{:S(2)}) copy-start(s32[8,128]{1,0:T(8,128)} %get-tuple-element.45) | copy-start | bytes 12292
  14.2 17.7 %copy-start.12 = (f32[1024]{0:T(1024)S(1)}, f32[1024]{0:T(1024)}, u32[]{:S(2)}) copy-start(f32[1024]{0:T(1024)} %param.15) | copy-start | bytes 12292
  14.2 17.7 %copy-start.13 = (s32[1024]{0:T(1024)S(1)}, s32[1024]{0:T(1024)}, u32[]{:S(2)}) copy-start(s32[1024]{0:T(1024)} %param.12) | copy-start | bytes 12292
  14.2 7.6 %collective-permute-start.2 = (f32[80,128]{1,0:T(8,128)}, f32[80,128]{1,0:T(8,128)S(1)}, u32[]{:S(2)}, u32[]{:S(2)}) collective-permute-start(f32[80,128]{1,0:T(8,128)} %get-tuple-element.37), channel_id=1, source_target_pairs={{0,3},{1,0},{2,1},{3,2},{4,7},{5,4},{6,5},{7,6},{8,11},{9,8},{10,9... | collective-permute-start | bytes 122888 | tf_op jit(solution)/shard_map/ppermute | solution.py:30
  16.8 5.0 %collective-permute-start.1 = (f32[80,128]{1,0:T(8,128)}, f32[80,128]{1,0:T(8,128)S(1)}, u32[]{:S(2)}, u32[]{:S(2)}) collective-permute-start(f32[80,128]{1,0:T(8,128)} %get-tuple-element.37), channel_id=1, source_target_pairs={{0,2},{1,3},{2,0},{3,1},{4,6},{5,7},{6,4},{7,5},{8,10},{9,11},{10,... | collective-permute-start | bytes 122888 | tf_op jit(solution)/shard_map/ppermute | solution.py:30
  17.3 4.5 %collective-permute-start = (f32[80,128]{1,0:T(8,128)}, f32[80,128]{1,0:T(8,128)S(1)}, u32[]{:S(2)}, u32[]{:S(2)}) collective-permute-start(f32[80,128]{1,0:T(8,128)} %get-tuple-element.37), channel_id=1, source_target_pairs={{0,1},{1,2},{2,3},{3,0},{4,5},{5,6},{6,7},{7,4},{8,9},{9,10},{10,1... | collective-permute-start | bytes 122888 | tf_op jit(solution)/shard_map/ppermute | solution.py:30
  21.8 18.0 %copy-start.10 = (s32[1024]{0:T(1024)S(1)}, s32[1024]{0:T(1024)}, u32[]{:S(2)}) copy-start(s32[1024]{0:T(1024)} %param.11) | copy-start | bytes 12292
  21.9 4.2 %collective-permute-start.3 = (f32[320,128]{1,0:T(8,128)S(1)}, f32[320,128]{1,0:T(8,128)S(1)}, u32[]{:S(2)}, u32[]{:S(2)}) collective-permute-start(f32[320,128]{1,0:T(8,128)S(1)} %get-tuple-element.72), channel_id=1, source_target_pairs={{0,4},{1,5},{2,6},{3,7},{4,8},{5,9},{6,10},{7,11},{8,12},{9,13},{1... | collective-permute-start | bytes 491528 | tf_op jit(solution)/shard_map/ppermute | solution.py:30
  21.9 5.8 %collective-permute-start.4 = (f32[320,128]{1,0:T(8,128)S(1)}, f32[320,128]{1,0:T(8,128)S(1)}, u32[]{:S(2)}, u32[]{:S(2)}) collective-permute-start(f32[320,128]{1,0:T(8,128)S(1)} %get-tuple-element.72), channel_id=1, source_target_pairs={{0,8},{1,9},{2,10},{3,11},{4,12},{5,13},{6,14},{7,15},{8,0},{9,1},... | collective-permute-start | bytes 491528 | tf_op jit(solution)/shard_map/ppermute | solution.py:30
  23.8 6.9 %collective-permute-start.5 = (f32[320,128]{1,0:T(8,128)S(1)}, f32[320,128]{1,0:T(8,128)S(1)}, u32[]{:S(2)}, u32[]{:S(2)}) collective-permute-start(f32[320,128]{1,0:T(8,128)S(1)} %get-tuple-element.72), channel_id=1, source_target_pairs={{0,12},{1,13},{2,14},{3,15},{4,0},{5,1},{6,2},{7,3},{8,4},{9,5},{1... | collective-permute-start | bytes 491528 | tf_op jit(solution)/shard_map/ppermute | solution.py:30
  30.7 3.4 %copy-start.6 = (f32[1280,128]{1,0:T(8,128)}, f32[1280,128]{1,0:T(8,128)S(1)}, u32[]{:S(2)}) copy-start(f32[1280,128]{1,0:T(8,128)S(1)} %constant_dynamic-update-slice_fusion.4.crossing_ref) | copy-start | bytes 1966084
  30.7 18.3 %copy-start.15 = (f32[72,768]{1,0:T(8,128)S(1)}, f32[72,768]{1,0:T(8,128)}, u32[]{:S(2)}) copy-start(f32[72,768]{1,0:T(8,128)} %get-tuple-element.49) | copy-start | bytes 663556
  30.7 27.9 %copy-start.14 = (f32[72,768]{1,0:T(8,128)S(1)}, f32[72,768]{1,0:T(8,128)}, u32[]{:S(2)}) copy-start(f32[72,768]{1,0:T(8,128)} %get-tuple-element.50) | copy-start | bytes 663556
  31.9 39.0 %copy-start.11 = (f32[1024]{0:T(1024)}, f32[1024]{0:T(1024)S(1)}, u32[]{:S(2)}) copy-start(f32[1024]{0:T(1024)S(1)} %convert_multiply_fusion) | copy-start | bytes 12292
  37.1 33.8 %copy-start.2 = (f32[768,128]{1,0:T(8,128)S(1)}, f32[768,128]{1,0:T(8,128)}, u32[]{:S(2)}) copy-start(f32[768,128]{1,0:T(8,128)} %order.1) | copy-start | bytes 1179652
  37.1 8.3 %collective-permute-start.7 = (f32[768,128]{1,0:T(8,128)}, f32[768,128]{1,0:T(8,128)S(1)}, u32[]{:S(2)}, u32[]{:S(2)}) collective-permute-start(f32[768,128]{1,0:T(8,128)} %order.1), channel_id=1, source_target_pairs={{0,96},{1,97},{2,98},{3,99},{4,100},{5,101},{6,102},{7,103},{8,104... | collective-permute-start | bytes 1179656 | tf_op jit(solution)/shard_map/ppermute | solution.py:30
  39.8 8.7 %collective-permute-start.6 = (f32[768,128]{1,0:T(8,128)}, f32[768,128]{1,0:T(8,128)S(1)}, u32[]{:S(2)}, u32[]{:S(2)}) collective-permute-start(f32[768,128]{1,0:T(8,128)} %order.1), channel_id=1, source_target_pairs={{0,32},{1,33},{2,34},{3,35},{4,36},{5,37},{6,38},{7,39},{8,40},{9,... | collective-permute-start | bytes 1179656 | tf_op jit(solution)/shard_map/ppermute | solution.py:30
  41.0 29.9 %copy-start.5 = (s32[16,72]{1,0:T(8,128)}, s32[16,72]{1,0:T(8,128)S(1)}, u32[]{:S(2)}) copy-start(s32[16,72]{1,0:T(8,128)S(1)} %pad_add_fusion.pi_slots_ref) | copy-start | bytes 13828
  48.6 22.2 %collective-permute-start.8 = (f32[768,128]{1,0:T(8,128)S(1)}, f32[768,128]{1,0:T(8,128)S(1)}, u32[]{:S(2)}, u32[]{:S(2)}) collective-permute-start(f32[768,128]{1,0:T(8,128)S(1)} %broadcast_select_fusion.1), channel_id=1, source_target_pairs={{0,32},{1,33},{2,34},{3,35},{4,36},{5,37},{6,38},{7,39},{8,40},{9,... | collective-permute-start | bytes 1179656 | tf_op jit(solution)/shard_map/ppermute | solution.py:30
  49.0 15.9 %collective-permute-start.9 = (f32[72,768]{1,0:T(8,128)S(1)}, f32[72,768]{1,0:T(8,128)S(1)}, u32[]{:S(2)}, u32[]{:S(2)}) collective-permute-start(f32[72,768]{1,0:T(8,128)S(1)} %copy-done.15), channel_id=1, source_target_pairs={{0,0},{1,1},{2,16},{3,17},{4,32},{5,33},{6,48},{7,49},{8,64},{9,65... | collective-permute-start | bytes 663560 | tf_op jit(solution)/shard_map/ppermute | solution.py:30
  58.6 12.2 %collective-permute-start.10 = (f32[72,768]{1,0:T(8,128)S(1)}, f32[72,768]{1,0:T(8,128)S(1)}, u32[]{:S(2)}, u32[]{:S(2)}) collective-permute-start(f32[72,768]{1,0:T(8,128)S(1)} %copy-done.14), channel_id=1, source_target_pairs={{0,1},{1,0},{2,17},{3,16},{4,33},{5,32},{6,49},{7,48},{8,65},{9,64... | collective-permute-start | bytes 663560 | tf_op jit(solution)/shard_map/ppermute | solution.py:30
  71.0 6.2 %copy-start = (f32[4,768,128]{2,1,0:T(8,128)}, f32[4,768,128]{2,1,0:T(8,128)S(1)}, u32[]{:S(2)}) copy-start(f32[4,768,128]{2,1,0:T(8,128)S(1)} %pad_maximum_fusion.mine_ref) | copy-start | bytes 4718596
  71.0 6.2 %collective-permute-start.13 = (f32[4,768,128]{2,1,0:T(8,128)S(1)}, f32[4,768,128]{2,1,0:T(8,128)S(1)}, u32[]{:S(2)}, u32[]{:S(2)}) collective-permute-start(f32[4,768,128]{2,1,0:T(8,128)S(1)} %pad_maximum_fusion.mine_ref), channel_id=1, source_target_pairs={{0,16},{1,17},{2,18},{3,19},{4,20},{5,21},{6,22},{7,23},{8,24},{9,... | collective-permute-start | bytes 4718600 | tf_op jit(solution)/shard_map/ppermute | solution.py:30
  74.2 15.6 %collective-permute-start.12 = (f32[144,768]{1,0:T(8,128)S(1)}, f32[144,768]{1,0:T(8,128)S(1)}, u32[]{:S(2)}, u32[]{:S(2)}) collective-permute-start(f32[144,768]{1,0:T(8,128)S(1)} %pad_maximum_fusion.2), channel_id=1, source_target_pairs={{0,96},{1,97},{2,98},{3,99},{4,100},{5,101},{6,102},{7,103},{8,104... | collective-permute-start | bytes 1327112 | tf_op jit(solution)/shard_map/ppermute | solution.py:30
  74.2 15.6 %collective-permute-start.11 = (f32[144,768]{1,0:T(8,128)S(1)}, f32[144,768]{1,0:T(8,128)S(1)}, u32[]{:S(2)}, u32[]{:S(2)}) collective-permute-start(f32[144,768]{1,0:T(8,128)S(1)} %pad_maximum_fusion.2), channel_id=1, source_target_pairs={{0,32},{1,33},{2,34},{3,35},{4,36},{5,37},{6,38},{7,39},{8,40},{9,... | collective-permute-start | bytes 1327112 | tf_op jit(solution)/shard_map/ppermute | solution.py:30
  77.2 1.3 copy-start.3
  89.9 8.5 %copy-start.1 = (f32[3,144,768]{2,1,0:T(8,128)}, f32[3,144,768]{2,1,0:T(8,128)S(1)}, u32[]{:S(2)}) copy-start(f32[3,144,768]{2,1,0:T(8,128)S(1)} %pad_maximum_fusion.1.mine_ref) | copy-start | bytes 3981316
  90.0 11.7 %collective-permute-start.15 = (f32[3,144,768]{2,1,0:T(8,128)S(1)}, f32[3,144,768]{2,1,0:T(8,128)S(1)}, u32[]{:S(2)}, u32[]{:S(2)}) collective-permute-start(f32[3,144,768]{2,1,0:T(8,128)S(1)} %pad_maximum_fusion.1.mine_ref), channel_id=1, source_target_pairs={{0,16},{1,17},{2,18},{3,19},{4,20},{5,21},{6,22},{7,23},{8,24},{9,... | collective-permute-start | bytes 3981320 | tf_op jit(solution)/shard_map/ppermute | solution.py:30
  90.4 8.0 %collective-permute-start.14 = (f32[144,768]{1,0:T(8,128)S(1)}, f32[144,768]{1,0:T(8,128)S(1)}, u32[]{:S(2)}, u32[]{:S(2)}) collective-permute-start(f32[144,768]{1,0:T(8,128)S(1)} %broadcast_select_fusion), channel_id=1, source_target_pairs={{0,32},{1,33},{2,34},{3,35},{4,36},{5,37},{6,38},{7,39},{8,40},{9,... | collective-permute-start | bytes 1327112 | tf_op jit(solution)/shard_map/ppermute | solution.py:30
  98.4 3.2 %copy-start.7 = (f32[144,768]{1,0:T(8,128)}, f32[144,768]{1,0:T(8,128)S(1)}, u32[]{:S(2)}) copy-start(f32[144,768]{1,0:T(8,128)S(1)} %collective-permute-done.14.far_ref) | copy-start | bytes 1327108
  98.4 3.2 %collective-permute-start.16 = (f32[144,768]{1,0:T(8,128)S(1)}, f32[144,768]{1,0:T(8,128)S(1)}, u32[]{:S(2)}, u32[]{:S(2)}) collective-permute-start(f32[144,768]{1,0:T(8,128)S(1)} %collective-permute-done.14.far_ref), channel_id=1, source_target_pairs={{0,16},{1,17},{2,18},{3,19},{4,20},{5,21},{6,22},{7,23},{8,24},{9,... | collective-permute-start | bytes 1327112 | tf_op jit(solution)/shard_map/ppermute | solution.py:30
  101.6 0.8 copy-start.8
  102.4 1.1 copy-start.4
Sparse Core Ops, SparseCore 0:
  30.9 73.9 all-gather.1

commit v3 on v2

--- a/solution.py
+++ b/solution.py
@@ -213,8 +213,15 @@
 
 
 def scale_kernel(
-    slots_ref, mine_ref, far_ref, mate_ref, far_mate_ref, wh_ref, wl_ref, out_ref, ph_ref, pl_ref
+    slots_ref, mine_ref, far_ref, mate_ref, far_mate_ref, high_ref, low_ref,
+    out_ref, ph_ref, pl_ref, wh_ref, wl_ref, sems,
 ):
+    copies = [
+        pltpu.make_async_copy(high_ref, wh_ref, sems.at[0]),
+        pltpu.make_async_copy(low_ref, wl_ref, sems.at[1]),
+    ]
+    for done in copies:
+        done.start()
     got = jnp.concatenate(
         [mine_ref[i] for i in range(3)] + [far_ref[...]] + [mate_ref[i] for i in range(3)] + [far_mate_ref[...]],
         axis=0,
@@ -224,6 +231,8 @@
         rows = slice(p * PANEL, (p + 1) * PANEL)
         pick = hot(iota((PANEL, KEXT), 0) + p * PANEL == slots_ref[...])
         ph_ref[rows, :], pl_ref[rows, :] = split(mm(pick, got_h) + mm(pick, got_l))
+    for done in copies:
+        done.wait()
     for p in range(PANELS):
         rows = slice(p * PANEL, (p + 1) * PANEL)
         deep = slice(0, (p + 1) * PANEL)
@@ -359,8 +368,16 @@
     strip_far_mate = shift(strip_far, core=1)
     scaled = pl.pallas_call(
         scale_kernel,
+        in_specs=[VM] * 5 + [ANY] * 2,
+        out_specs=VM,
         out_shape=jax.ShapeDtypeStruct((2 * SLOTS, cols_blk), BF16),
-        scratch_shapes=[pltpu.VMEM((SLOTS, cols_blk), BF16)] * 2,
+        scratch_shapes=[
+            pltpu.VMEM((SLOTS, cols_blk), BF16),
+            pltpu.VMEM((SLOTS, cols_blk), BF16),
+            pltpu.VMEM((SLOTS, SLOTS), BF16),
+            pltpu.VMEM((SLOTS, SLOTS), BF16),
+            pltpu.SemaphoreType.DMA((2,)),
+        ],
         compiler_params=PARAMS,
         name="scale",
     )(pair_slots, strip_mine, strip_far, strip_mate, strip_far_mate, w_high, w_low)

time: 151 us -> 150 us (level)
  no operation moved by 1% of the time
where the time goes in v3:
time: 150 us
  Pallas kernels  69.2 us (46%)
  waiting for transfers between devices  27.9 us (19%)
  starting transfers between devices  25.3 us (17%)
  between operations  14.4 us (10%)
  local copies, waits for them, and re-layouts  10.5 us (7%)
  other arithmetic  2.79 us (2%)
    pallas_call x1, Pallas kernels, body(): pl.pallas_call(update_kernel, grid=(rows_blk // tile,), in_specs=[pl.Bloc...  28.3 us
    ppermute x17, waiting for transfers between devices, permute(): return lax.ppermute(value, AXES, pairs)  27.9 us
    ppermute x17, starting transfers between devices, permute(): return lax.ppermute(value, AXES, pairs)  25.3 us
    pallas_call x1, Pallas kernels, body(): pl.pallas_call(scale_kernel, in_specs=[VM] * 5 + [ANY] * 2, out_specs=VM,...  11.6 us
    pallas_call x1, Pallas kernels, body(): pl.pallas_call(weight_kernel, out_shape=[square] * 4, compiler_params=PAR...  11.3 us
    pallas_call x1, Pallas kernels, body(): pl.pallas_call(expand_kernel, out_shape=jax.ShapeDtypeStruct((2 * KEXT, S...  7.94 us
    pallas_call x1, Pallas kernels, body(): pl.pallas_call(extract_kernel, in_specs=[VM, VM, VM, ANY], out_specs=[VM]...  6.96 us
    unnamed x38, local copies, waits for them, and re-layouts  4.06 us
  transfers between devices with their start and end apart: 18, of which 10 were waited for; matrix products, arithmetic and copies ran while one was open for 7% of the time, Pallas kernels for 23%

profile of v3, /device:TPU:97, one launch (start us, length us, event | category | flops | bytes accessed | tf_op | source)
XLA Modules:
  0.0 150.2 jit_solution(12610538562262961552)
XLA Ops:
  7.2 7.0 %extract.1 = (f32[72,1536]{1,0:T(8,128)}, f32[80,128]{1,0:T(8,128)}, f32[72,768]{1,0:T(8,128)}, f32[72,768]{1,0:T(8,128)}, s32[8,128]{1,0:T(8,128)}, /*index=5*/s32[8,128]{1,0:T(8,128)}) custom-call(s32[8,128]{1,0:T(8,128)} %bitcast.30, s32[1,8]{1,0:T(1,128)} %bitcast.35, f32[8,1536]{1,0:T(8,128)} %delayed_ref.1, f32[1536,768]{1,0:T(8,128)} %front_ref.3), custom_call_target="tpu_custom_call" | custom-call | tf_op jit(solution)/shard_map/extract/pallas_call | solution.py:273
  14.2 2.6 %collective-permute-start.2 = (f32[80,128]{1,0:T(8,128)}, f32[80,128]{1,0:T(8,128)S(1)}, u32[]{:S(2)}, u32[]{:S(2)}) collective-permute-start(f32[80,128]{1,0:T(8,128)} %get-tuple-element.37), channel_id=1, source_target_pairs={{0,3},{1,0},{2,1},{3,2},{4,7},{5,4},{6,5},{7,6},{8,11},{9,8},{10,9... | collective-permute-start | bytes 122888 | tf_op jit(solution)/shard_map/ppermute | solution.py:30
  16.8 0.5 collective-permute-start.1
  17.3 0.6 collective-permute-start
  17.9 0.8 constant_dynamic-update-slice_fusion.3
  18.7 3.1 %collective-permute-done = f32[80,128]{1,0:T(8,128)S(1)} collective-permute-done((f32[80,128]{1,0:T(8,128)}, f32[80,128]{1,0:T(8,128)S(1)}, u32[]{:S(2)}, u32[]{:S(2)}) %collective-permute-start) | collective-permute-done | bytes 40992 | tf_op jit(solution)/shard_map/ppermute | solution.py:30
  21.9 1.9 %collective-permute-start.4 = (f32[320,128]{1,0:T(8,128)S(1)}, f32[320,128]{1,0:T(8,128)S(1)}, u32[]{:S(2)}, u32[]{:S(2)}) collective-permute-start(f32[320,128]{1,0:T(8,128)S(1)} %get-tuple-element.72), channel_id=1, source_target_pairs={{0,8},{1,9},{2,10},{3,11},{4,12},{5,13},{6,14},{7,15},{8,0},{9,1},... | collective-permute-start | bytes 491528 | tf_op jit(solution)/shard_map/ppermute | solution.py:30
  23.8 2.3 %collective-permute-done.3 = f32[320,128]{1,0:T(8,128)S(1)} collective-permute-done((f32[320,128]{1,0:T(8,128)S(1)}, f32[320,128]{1,0:T(8,128)S(1)}, u32[]{:S(2)}, u32[]{:S(2)}) %collective-permute-start.3) | collective-permute-done | bytes 163872 | tf_op jit(solution)/shard_map/ppermute | solution.py:30
  26.1 1.6 %collective-permute-done.4 = f32[320,128]{1,0:T(8,128)S(1)} collective-permute-done((f32[320,128]{1,0:T(8,128)S(1)}, f32[320,128]{1,0:T(8,128)S(1)}, u32[]{:S(2)}, u32[]{:S(2)}) %collective-permute-start.4) | collective-permute-done | bytes 163872 | tf_op jit(solution)/shard_map/ppermute | solution.py:30
  27.7 2.9 %collective-permute-done.5 = f32[320,128]{1,0:T(8,128)S(1)} collective-permute-done((f32[320,128]{1,0:T(8,128)S(1)}, f32[320,128]{1,0:T(8,128)S(1)}, u32[]{:S(2)}, u32[]{:S(2)}) %collective-permute-start.5) | collective-permute-done | bytes 163872 | tf_op jit(solution)/shard_map/ppermute | solution.py:30
  30.8 0.1 pad.17.clone
  30.9 0.1 copy.25
  31.0 0.1 reshape.535
  31.2 0.6 gather_fusion
  31.9 0.7 pad_maximum_fusion.3
  32.7 0.6 gather_fusion.2
  33.3 0.1 add_add_fusion
  33.4 0.7 reshape.534.slots_ref
  34.1 3.1 %order.1 = f32[768,128]{1,0:T(8,128)} custom-call(s32[1,1280]{1,0:T(1,128)} %reshape.534.slots_ref, f32[1280,128]{1,0:T(8,128)} %copy-done.6), custom_call_target="tpu_custom_call" | custom-call | tf_op jit(solution)/shard_map/order/pallas_call | solution.py:303
  37.1 2.7 %collective-permute-start.7 = (f32[768,128]{1,0:T(8,128)}, f32[768,128]{1,0:T(8,128)S(1)}, u32[]{:S(2)}, u32[]{:S(2)}) collective-permute-start(f32[768,128]{1,0:T(8,128)} %order.1), channel_id=1, source_target_pairs={{0,96},{1,97},{2,98},{3,99},{4,100},{5,101},{6,102},{7,103},{8,104... | collective-permute-start | bytes 1179656 | tf_op jit(solution)/shard_map/ppermute | solution.py:30
  39.8 0.5 compare_reduce_fusion.1
  40.4 0.6 sub.170.col_ref
  41.0 0.6 gather_fusion.3
  41.6 0.7 reshape.536.slots_ref
  42.3 1.0 compare_reduce_fusion
  43.3 1.1 gather_fusion.1
  44.4 1.0 collective-permute-done.7
  45.4 3.1 %collective-permute-done.6 = f32[768,128]{1,0:T(8,128)S(1)} collective-permute-done((f32[768,128]{1,0:T(8,128)}, f32[768,128]{1,0:T(8,128)S(1)}, u32[]{:S(2)}, u32[]{:S(2)}) %collective-permute-start.6) | collective-permute-done | bytes 393248 | tf_op jit(solution)/shard_map/ppermute | solution.py:30
  48.6 0.4 collective-permute-start.8
  49.0 9.6 %collective-permute-start.9 = (f32[72,768]{1,0:T(8,128)S(1)}, f32[72,768]{1,0:T(8,128)S(1)}, u32[]{:S(2)}, u32[]{:S(2)}) collective-permute-start(f32[72,768]{1,0:T(8,128)S(1)} %copy-done.15), channel_id=1, source_target_pairs={{0,0},{1,1},{2,16},{3,17},{4,32},{5,33},{6,48},{7,49},{8,64},{9,65... | collective-permute-start | bytes 663560 | tf_op jit(solution)/shard_map/ppermute | solution.py:30
  58.7 6.2 %collective-permute-done.9 = f32[72,768]{1,0:T(8,128)S(1)} collective-permute-done((f32[72,768]{1,0:T(8,128)S(1)}, f32[72,768]{1,0:T(8,128)S(1)}, u32[]{:S(2)}, u32[]{:S(2)}) %collective-permute-start.9) | collective-permute-done | bytes 221216 | tf_op jit(solution)/shard_map/ppermute | solution.py:30
  64.8 6.0 %collective-permute-done.10 = f32[72,768]{1,0:T(8,128)S(1)} collective-permute-done((f32[72,768]{1,0:T(8,128)S(1)}, f32[72,768]{1,0:T(8,128)S(1)}, u32[]{:S(2)}, u32[]{:S(2)}) %collective-permute-start.10) | collective-permute-done | bytes 221216 | tf_op jit(solution)/shard_map/ppermute | solution.py:30
  70.9 0.1 pad_maximum_fusion.mine_ref
  71.0 3.2 %collective-permute-start.13 = (f32[4,768,128]{2,1,0:T(8,128)S(1)}, f32[4,768,128]{2,1,0:T(8,128)S(1)}, u32[]{:S(2)}, u32[]{:S(2)}) collective-permute-start(f32[4,768,128]{2,1,0:T(8,128)S(1)} %pad_maximum_fusion.mine_ref), channel_id=1, source_target_pairs={{0,16},{1,17},{2,18},{3,19},{4,20},{5,21},{6,22},{7,23},{8,24},{9,... | collective-permute-start | bytes 4718600 | tf_op jit(solution)/shard_map/ppermute | solution.py:30
  74.2 1.5 collective-permute-start.11
  75.7 1.6 %collective-permute-done.13.mate_ref = f32[4,768,128]{2,1,0:T(8,128)S(1)} collective-permute-done((f32[4,768,128]{2,1,0:T(8,128)S(1)}, f32[4,768,128]{2,1,0:T(8,128)S(1)}, u32[]{:S(2)}, u32[]{:S(2)}) %collective-permute-start.13) | collective-permute-done | bytes 1572896 | tf_op jit(solution)/shard_map/ppermute | solution.py:30
  77.2 1.2 copy-done.3
  78.5 11.3 %weights.1 = (bf16[1024,1024]{1,0:T(8,128)(2,1)}, bf16[1024,1024]{1,0:T(8,128)(2,1)}, bf16[1024,1024]{1,0:T(8,128)(2,1)}, bf16[1024,1024]{1,0:T(8,128)(2,1)}) custom-call(s32[8,128]{1,0:T(8,128)} %gather_fusion.1, f32[4,768,128]{2,1,0:T(8,128)} %copy-done, f32[4,768,128]{2,1,0:T(8,128)} %copy-done.3, f32[4,256,256]{2,1,0:T(8,128)} %linv_ref.1, ...), custom_call_target="tpu_custom_call" | custom-call | tf_op jit(solution)/shard_map/weights/pallas_call | solution.py:348
  89.8 0.1 pad_maximum_fusion.1.mine_ref
  90.0 0.4 collective-permute-start.15
  90.5 7.9 %expand.1.wide_ref = bf16[2304,1024]{1,0:T(8,128)(2,1)} custom-call(s32[16,72]{1,0:T(8,128)} %copy-done.5, bf16[1024,1024]{1,0:T(8,128)(2,1)} %get-tuple-element.63.dh_ref, bf16[1024,1024]{1,0:T(8,128)(2,1)} %get-tuple-element.64.dl_ref), custom_call_target="tpu_custom_call" | custom-call | tf_op jit(solution)/shard_map/expand/pallas_call | solution.py:361
  98.4 1.8 %collective-permute-start.16 = (f32[144,768]{1,0:T(8,128)S(1)}, f32[144,768]{1,0:T(8,128)S(1)}, u32[]{:S(2)}, u32[]{:S(2)}) collective-permute-start(f32[144,768]{1,0:T(8,128)S(1)} %collective-permute-done.14.far_ref), channel_id=1, source_target_pairs={{0,16},{1,17},{2,18},{3,19},{4,20},{5,21},{6,22},{7,23},{8,24},{9,... | collective-permute-start | bytes 1327112 | tf_op jit(solution)/shard_map/ppermute | solution.py:30
  100.2 1.3 copy.26.row_ref
  101.4 0.2 collective-permute-done.16.far_mate_ref
  101.6 0.7 copy-done.8
  102.4 1.1 copy-done.4
  103.4 11.6 %scale.1.scaled_ref = bf16[2048,768]{1,0:T(8,128)(2,1)} custom-call(s32[1,1152]{1,0:T(1,128)} %reshape.536.slots_ref, f32[3,144,768]{2,1,0:T(8,128)} %copy-done.1, f32[144,768]{1,0:T(8,128)} %copy-done.7, f32[3,144,768]{2,1,0:T(8,128)} %copy-done.4, f32[144,768]{1,0:T(8,128)} %copy-done.8, bf16[1024,1024]{1,0:T(8,128)(2,1)} %get-tuple-element.68.high_ref, ...), custom_call_target="tpu_custom_call" | custom-call | tf_op jit(solution)/shard_map/scale/pallas_call | solution.py:369
  115.1 28.3 %update.1 = (f32[1536,768]{1,0:T(8,128)}, f32[1536,1024]{1,0:T(8,128)}) custom-call(f32[1152,1536]{1,0:T(8,128)} %all-gather.2.cloned.1.call-done.piece_ref, bf16[2304,1024]{1,0:T(8,128)(2,1)} %expand.1.wide_ref, bf16[2048,768]{1,0:T(8,128)(2,1)} %scale.1.scaled_ref, f32[1536,768]{1,0:T(8,128)} %front_ref.3, f32[1536,1]{1,0:T(8,128)} %copy.26.row_ref, ...), custom_call_target="tpu_custom_call" | custom-call | tf_op jit(solution)/shard_map/update/pallas_call | solution.py:386
  (75 shorter events, 1.0 us)
Async XLA Ops:
  7.2 107.9 %all-gather.2.cloned.1.call-start = ((), (), s32[]{:S(2)}) async-start(), calls=%async_computation | async-start | bytes 7520256 | tf_op jit(solution)/shard_map/all_gather | solution.py:293
  14.2 16.9 %copy-start.9 = (s32[8,128]{1,0:T(8,128)S(1)}, s32[8,128]{1,0:T(8,128)}, u32[]{:S(2)}) copy-start(s32[8,128]{1,0:T(8,128)} %get-tuple-element.45) | copy-start | bytes 12292
  14.2 17.7 %copy-start.12 = (f32[1024]{0:T(1024)S(1)}, f32[1024]{0:T(1024)}, u32[]{:S(2)}) copy-start(f32[1024]{0:T(1024)} %param.15) | copy-start | bytes 12292
  14.2 17.7 %copy-start.13 = (s32[1024]{0:T(1024)S(1)}, s32[1024]{0:T(1024)}, u32[]{:S(2)}) copy-start(s32[1024]{0:T(1024)} %param.12) | copy-start | bytes 12292
  14.2 7.6 %collective-permute-start.2 = (f32[80,128]{1,0:T(8,128)}, f32[80,128]{1,0:T(8,128)S(1)}, u32[]{:S(2)}, u32[]{:S(2)}) collective-permute-start(f32[80,128]{1,0:T(8,128)} %get-tuple-element.37), channel_id=1, source_target_pairs={{0,3},{1,0},{2,1},{3,2},{4,7},{5,4},{6,5},{7,6},{8,11},{9,8},{10,9... | collective-permute-start | bytes 122888 | tf_op jit(solution)/shard_map/ppermute | solution.py:30
  16.8 5.0 %collective-permute-start.1 = (f32[80,128]{1,0:T(8,128)}, f32[80,128]{1,0:T(8,128)S(1)}, u32[]{:S(2)}, u32[]{:S(2)}) collective-permute-start(f32[80,128]{1,0:T(8,128)} %get-tuple-element.37), channel_id=1, source_target_pairs={{0,2},{1,3},{2,0},{3,1},{4,6},{5,7},{6,4},{7,5},{8,10},{9,11},{10,... | collective-permute-start | bytes 122888 | tf_op jit(solution)/shard_map/ppermute | solution.py:30
  17.3 4.5 %collective-permute-start = (f32[80,128]{1,0:T(8,128)}, f32[80,128]{1,0:T(8,128)S(1)}, u32[]{:S(2)}, u32[]{:S(2)}) collective-permute-start(f32[80,128]{1,0:T(8,128)} %get-tuple-element.37), channel_id=1, source_target_pairs={{0,1},{1,2},{2,3},{3,0},{4,5},{5,6},{6,7},{7,4},{8,9},{9,10},{10,1... | collective-permute-start | bytes 122888 | tf_op jit(solution)/shard_map/ppermute | solution.py:30
  21.8 18.0 %copy-start.10 = (s32[1024]{0:T(1024)S(1)}, s32[1024]{0:T(1024)}, u32[]{:S(2)}) copy-start(s32[1024]{0:T(1024)} %param.11) | copy-start | bytes 12292
  21.9 4.2 %collective-permute-start.3 = (f32[320,128]{1,0:T(8,128)S(1)}, f32[320,128]{1,0:T(8,128)S(1)}, u32[]{:S(2)}, u32[]{:S(2)}) collective-permute-start(f32[320,128]{1,0:T(8,128)S(1)} %get-tuple-element.72), channel_id=1, source_target_pairs={{0,4},{1,5},{2,6},{3,7},{4,8},{5,9},{6,10},{7,11},{8,12},{9,13},{1... | collective-permute-start | bytes 491528 | tf_op jit(solution)/shard_map/ppermute | solution.py:30
  21.9 5.8 %collective-permute-start.4 = (f32[320,128]{1,0:T(8,128)S(1)}, f32[320,128]{1,0:T(8,128)S(1)}, u32[]{:S(2)}, u32[]{:S(2)}) collective-permute-start(f32[320,128]{1,0:T(8,128)S(1)} %get-tuple-element.72), channel_id=1, source_target_pairs={{0,8},{1,9},{2,10},{3,11},{4,12},{5,13},{6,14},{7,15},{8,0},{9,1},... | collective-permute-start | bytes 491528 | tf_op jit(solution)/shard_map/ppermute | solution.py:30
  23.8 6.9 %collective-permute-start.5 = (f32[320,128]{1,0:T(8,128)S(1)}, f32[320,128]{1,0:T(8,128)S(1)}, u32[]{:S(2)}, u32[]{:S(2)}) collective-permute-start(f32[320,128]{1,0:T(8,128)S(1)} %get-tuple-element.72), channel_id=1, source_target_pairs={{0,12},{1,13},{2,14},{3,15},{4,0},{5,1},{6,2},{7,3},{8,4},{9,5},{1... | collective-permute-start | bytes 491528 | tf_op jit(solution)/shard_map/ppermute | solution.py:30
  30.7 3.4 %copy-start.6 = (f32[1280,128]{1,0:T(8,128)}, f32[1280,128]{1,0:T(8,128)S(1)}, u32[]{:S(2)}) copy-start(f32[1280,128]{1,0:T(8,128)S(1)} %constant_dynamic-update-slice_fusion.4.crossing_ref) | copy-start | bytes 1966084
  30.7 18.3 %copy-start.15 = (f32[72,768]{1,0:T(8,128)S(1)}, f32[72,768]{1,0:T(8,128)}, u32[]{:S(2)}) copy-start(f32[72,768]{1,0:T(8,128)} %get-tuple-element.49) | copy-start | bytes 663556
  30.7 27.9 %copy-start.14 = (f32[72,768]{1,0:T(8,128)S(1)}, f32[72,768]{1,0:T(8,128)}, u32[]{:S(2)}) copy-start(f32[72,768]{1,0:T(8,128)} %get-tuple-element.50) | copy-start | bytes 663556
  31.9 39.0 %copy-start.11 = (f32[1024]{0:T(1024)}, f32[1024]{0:T(1024)S(1)}, u32[]{:S(2)}) copy-start(f32[1024]{0:T(1024)S(1)} %convert_multiply_fusion) | copy-start | bytes 12292
  37.1 33.8 %copy-start.2 = (f32[768,128]{1,0:T(8,128)S(1)}, f32[768,128]{1,0:T(8,128)}, u32[]{:S(2)}) copy-start(f32[768,128]{1,0:T(8,128)} %order.1) | copy-start | bytes 1179652
  37.1 8.3 %collective-permute-start.7 = (f32[768,128]{1,0:T(8,128)}, f32[768,128]{1,0:T(8,128)S(1)}, u32[]{:S(2)}, u32[]{:S(2)}) collective-permute-start(f32[768,128]{1,0:T(8,128)} %order.1), channel_id=1, source_target_pairs={{0,96},{1,97},{2,98},{3,99},{4,100},{5,101},{6,102},{7,103},{8,104... | collective-permute-start | bytes 1179656 | tf_op jit(solution)/shard_map/ppermute | solution.py:30
  39.8 8.7 %collective-permute-start.6 = (f32[768,128]{1,0:T(8,128)}, f32[768,128]{1,0:T(8,128)S(1)}, u32[]{:S(2)}, u32[]{:S(2)}) collective-permute-start(f32[768,128]{1,0:T(8,128)} %order.1), channel_id=1, source_target_pairs={{0,32},{1,33},{2,34},{3,35},{4,36},{5,37},{6,38},{7,39},{8,40},{9,... | collective-permute-start | bytes 1179656 | tf_op jit(solution)/shard_map/ppermute | solution.py:30
  41.0 29.9 %copy-start.5 = (s32[16,72]{1,0:T(8,128)}, s32[16,72]{1,0:T(8,128)S(1)}, u32[]{:S(2)}) copy-start(s32[16,72]{1,0:T(8,128)S(1)} %pad_add_fusion.pi_slots_ref) | copy-start | bytes 13828
  48.6 22.2 %collective-permute-start.8 = (f32[768,128]{1,0:T(8,128)S(1)}, f32[768,128]{1,0:T(8,128)S(1)}, u32[]{:S(2)}, u32[]{:S(2)}) collective-permute-start(f32[768,128]{1,0:T(8,128)S(1)} %broadcast_select_fusion.1), channel_id=1, source_target_pairs={{0,32},{1,33},{2,34},{3,35},{4,36},{5,37},{6,38},{7,39},{8,40},{9,... | collective-permute-start | bytes 1179656 | tf_op jit(solution)/shard_map/ppermute | solution.py:30
  49.0 15.9 %collective-permute-start.9 = (f32[72,768]{1,0:T(8,128)S(1)}, f32[72,768]{1,0:T(8,128)S(1)}, u32[]{:S(2)}, u32[]{:S(2)}) collective-permute-start(f32[72,768]{1,0:T(8,128)S(1)} %copy-done.15), channel_id=1, source_target_pairs={{0,0},{1,1},{2,16},{3,17},{4,32},{5,33},{6,48},{7,49},{8,64},{9,65... | collective-permute-start | bytes 663560 | tf_op jit(solution)/shard_map/ppermute | solution.py:30
  58.6 12.2 %collective-permute-start.10 = (f32[72,768]{1,0:T(8,128)S(1)}, f32[72,768]{1,0:T(8,128)S(1)}, u32[]{:S(2)}, u32[]{:S(2)}) collective-permute-start(f32[72,768]{1,0:T(8,128)S(1)} %copy-done.14), channel_id=1, source_target_pairs={{0,1},{1,0},{2,17},{3,16},{4,33},{5,32},{6,49},{7,48},{8,65},{9,64... | collective-permute-start | bytes 663560 | tf_op jit(solution)/shard_map/ppermute | solution.py:30
  71.0 6.2 %copy-start = (f32[4,768,128]{2,1,0:T(8,128)}, f32[4,768,128]{2,1,0:T(8,128)S(1)}, u32[]{:S(2)}) copy-start(f32[4,768,128]{2,1,0:T(8,128)S(1)} %pad_maximum_fusion.mine_ref) | copy-start | bytes 4718596
  71.0 6.2 %collective-permute-start.13 = (f32[4,768,128]{2,1,0:T(8,128)S(1)}, f32[4,768,128]{2,1,0:T(8,128)S(1)}, u32[]{:S(2)}, u32[]{:S(2)}) collective-permute-start(f32[4,768,128]{2,1,0:T(8,128)S(1)} %pad_maximum_fusion.mine_ref), channel_id=1, source_target_pairs={{0,16},{1,17},{2,18},{3,19},{4,20},{5,21},{6,22},{7,23},{8,24},{9,... | collective-permute-start | bytes 4718600 | tf_op jit(solution)/shard_map/ppermute | solution.py:30
  74.2 15.6 %collective-permute-start.12 = (f32[144,768]{1,0:T(8,128)S(1)}, f32[144,768]{1,0:T(8,128)S(1)}, u32[]{:S(2)}, u32[]{:S(2)}) collective-permute-start(f32[144,768]{1,0:T(8,128)S(1)} %pad_maximum_fusion.2), channel_id=1, source_target_pairs={{0,96},{1,97},{2,98},{3,99},{4,100},{5,101},{6,102},{7,103},{8,104... | collective-permute-start | bytes 1327112 | tf_op jit(solution)/shard_map/ppermute | solution.py:30
  74.2 15.6 %collective-permute-start.11 = (f32[144,768]{1,0:T(8,128)S(1)}, f32[144,768]{1,0:T(8,128)S(1)}, u32[]{:S(2)}, u32[]{:S(2)}) collective-permute-start(f32[144,768]{1,0:T(8,128)S(1)} %pad_maximum_fusion.2), channel_id=1, source_target_pairs={{0,32},{1,33},{2,34},{3,35},{4,36},{5,37},{6,38},{7,39},{8,40},{9,... | collective-permute-start | bytes 1327112 | tf_op jit(solution)/shard_map/ppermute | solution.py:30
  77.2 1.3 copy-start.3
  89.9 8.5 %copy-start.1 = (f32[3,144,768]{2,1,0:T(8,128)}, f32[3,144,768]{2,1,0:T(8,128)S(1)}, u32[]{:S(2)}) copy-start(f32[3,144,768]{2,1,0:T(8,128)S(1)} %pad_maximum_fusion.1.mine_ref) | copy-start | bytes 3981316
  90.0 11.7 %collective-permute-start.15 = (f32[3,144,768]{2,1,0:T(8,128)S(1)}, f32[3,144,768]{2,1,0:T(8,128)S(1)}, u32[]{:S(2)}, u32[]{:S(2)}) collective-permute-start(f32[3,144,768]{2,1,0:T(8,128)S(1)} %pad_maximum_fusion.1.mine_ref), channel_id=1, source_target_pairs={{0,16},{1,17},{2,18},{3,19},{4,20},{5,21},{6,22},{7,23},{8,24},{9,... | collective-permute-start | bytes 3981320 | tf_op jit(solution)/shard_map/ppermute | solution.py:30
  90.4 8.0 %collective-permute-start.14 = (f32[144,768]{1,0:T(8,128)S(1)}, f32[144,768]{1,0:T(8,128)S(1)}, u32[]{:S(2)}, u32[]{:S(2)}) collective-permute-start(f32[144,768]{1,0:T(8,128)S(1)} %broadcast_select_fusion), channel_id=1, source_target_pairs={{0,32},{1,33},{2,34},{3,35},{4,36},{5,37},{6,38},{7,39},{8,40},{9,... | collective-permute-start | bytes 1327112 | tf_op jit(solution)/shard_map/ppermute | solution.py:30
  98.4 3.2 %copy-start.7 = (f32[144,768]{1,0:T(8,128)}, f32[144,768]{1,0:T(8,128)S(1)}, u32[]{:S(2)}) copy-start(f32[144,768]{1,0:T(8,128)S(1)} %collective-permute-done.14.far_ref) | copy-start | bytes 1327108
  98.4 3.2 %collective-permute-start.16 = (f32[144,768]{1,0:T(8,128)S(1)}, f32[144,768]{1,0:T(8,128)S(1)}, u32[]{:S(2)}, u32[]{:S(2)}) collective-permute-start(f32[144,768]{1,0:T(8,128)S(1)} %collective-permute-done.14.far_ref), channel_id=1, source_target_pairs={{0,16},{1,17},{2,18},{3,19},{4,20},{5,21},{6,22},{7,23},{8,24},{9,... | collective-permute-start | bytes 1327112 | tf_op jit(solution)/shard_map/ppermute | solution.py:30
  101.6 0.8 copy-start.8
  102.4 1.1 copy-start.4
Sparse Core Ops, SparseCore 0:
  30.9 73.9 all-gather.1
